TPU v7x, 32 devices: a whole 2x2x4 slice. The times are simulated.
32 devices in a mesh: dp: 8 (over z, y), seq: 4 (over x, core).
Axes of the slice: x: 2, y: 2, z: 4, core: 2. Of those that a mesh axis runs over, the one named last changes fastest.
Arguments:
- inputs: bfloat16 [8, 1024, 768], P('dp', 'seq'), may hold values from -6 to 6
- attn_gain: float32 [768], P('dp'), may hold values from 0.5 to 1.5
- qkv_weight: float32 [768, 12, 3, 64], P('dp'), may hold values from -0.21875 to 0.21875
- out_weight: float32 [768, 768], P('dp'), may hold values from -3.5 to 3.5
- ffn_gain: float32 [768], P('dp'), may hold values from 0.5 to 1.5
- router_weight: float32 [768, 3], P('dp'), may hold values from -0.15625 to 0.15625
- expert_in: float32 [3, 768, 4096], P(None, 'dp'), may hold values from -0.21875 to 0.21875
- expert_out: float32 [3, 2048, 768], P(None, 'dp'), may hold values from -0.5 to 0.5
- shared_in: float32 [768, 4096], P('dp'), may hold values from -0.21875 to 0.21875
- shared_out: float32 [2048, 768], P('dp'), may hold values from -0.25 to 0.25
- routes: int32 [8, 1024, 2], P('dp', 'seq'), may hold values from 0 to 2, as said below
- slot_index: int32 [8, 1024, 2], P('dp', 'seq'), may hold values from 0 to 191, as said below
- cotangent: bfloat16 [8, 1024, 768], P('dp', 'seq'), may hold values from -6 to 6
Outputs:
- output: bfloat16 [8, 1024, 768], P('dp', 'seq')
- input_grad: float32 [8, 1024, 768], P('dp', 'seq')
- attn_gain_grad: float32 [768], P('dp')
- qkv_weight_grad: float32 [768, 12, 3, 64], P('dp')
- out_weight_grad: float32 [768, 768], P('dp')
- ffn_gain_grad: float32 [768], P('dp')
- router_weight_grad: float32 [768, 3], P('dp')
- expert_in_grad: float32 [3, 768, 4096], P(None, 'dp')
- expert_out_grad: float32 [3, 2048, 768], P(None, 'dp')
- shared_in_grad: float32 [768, 4096], P('dp')
- shared_out_grad: float32 [2048, 768], P('dp')
Inputs may be any that keep to these rules, and one draw needn't show every extreme that they name: `routes`: A token's 2 experts differ. Within the tokens of one device (aligned blocks of 256 tokens of a sequence), no expert is named more than 192 times, one expert exactly 192 times, and every expert at least once. `slot_index`: within the tokens of one device, the slots of an expert named n times are 0 to n - 1, each once.
All inputs are finite; a program needn't handle non-finite values.
Results may differ from a plain program's by a relative error of at most 0.02.
The roundings to bfloat16 on the way count: a program that leaves them out, or rounds other values in their place, can miss the bound.
Values may be sent and summed in bfloat16 or wider, within the bound.
A program may use at most 160 MiB of HBM per device.

v0:
```python
import jax
import jax.numpy as jnp
from jax import lax
from jax.sharding import PartitionSpec as P

D = 768
HEADS = 12
HEAD_DIM = 64
FF = 2048
EXPERTS = 3
TOP = 2
ATT_BLOCK = 256
CAP = 192


EPSILON = 1e-05


def rotary_tables(positions):
    half_dim = HEAD_DIM // 2
    frequency = 10000.0 ** (-jnp.arange(half_dim, dtype=jnp.float32) / half_dim)
    angles = positions.astype(jnp.float32)[:, None] * frequency[None, :]
    return (jnp.cos(angles), jnp.sin(angles))


def rotate(values, cos_table, sine_table):
    half_dim = values.shape[-1] // 2
    first_half = values[..., :half_dim]
    second_half = values[..., half_dim:]
    cos_heads = cos_table[:, None, :]
    sine_heads = sine_table[:, None, :]
    return jnp.concatenate(
        [
            first_half * cos_heads - second_half * sine_heads,
            second_half * cos_heads + first_half * sine_heads,
        ],
        axis=-1,
    )


def unrotate(values, cos_table, sine_table):
    half_dim = values.shape[-1] // 2
    first_half = values[..., :half_dim]
    second_half = values[..., half_dim:]
    cos_heads = cos_table[:, None, :]
    sine_heads = sine_table[:, None, :]
    return jnp.concatenate(
        [
            first_half * cos_heads + second_half * sine_heads,
            second_half * cos_heads - first_half * sine_heads,
        ],
        axis=-1,
    )


def silu_grads(gate_in, up_in, upstream):
    sigmoid = jax.nn.sigmoid(gate_in)
    swish = gate_in * sigmoid
    slope = sigmoid * (1.0 + gate_in * (1.0 - sigmoid))
    return jnp.concatenate([upstream * up_in * slope, upstream * swish], axis=-1)


def block_mask(row_start, block_rows, length):
    query_block = (row_start + jnp.arange(block_rows, dtype=jnp.int32)) // ATT_BLOCK
    key_block = jnp.arange(length, dtype=jnp.int32) // ATT_BLOCK
    return key_block[None, :] <= query_block[:, None]


def attend_heads(received):
    packed = received[:, 0]
    length = packed.shape[0]
    heads_here = packed.shape[1]
    queries = packed[..., :HEAD_DIM]
    keys_all = packed[..., HEAD_DIM : 2 * HEAD_DIM]
    values_all = packed[..., 2 * HEAD_DIM :]
    block_rows = min(512, length)
    block_count = length // block_rows
    score_scale = HEAD_DIM ** (-0.5)

    def one_block(element):
        query_rows, row_start = element
        scores = (
            jnp.einsum("qhe,khe->hqk", query_rows, keys_all, preferred_element_type=jnp.float32)
            * score_scale
        )
        scores = jnp.where(block_mask(row_start, block_rows, length)[None], scores, -1e30)
        largest = jnp.max(scores, axis=-1, keepdims=True)
        weights_exp = jnp.exp(scores - largest)
        totals = jnp.sum(weights_exp, axis=-1, keepdims=True)
        attn_probs = (weights_exp / totals).astype(jnp.bfloat16)
        mixed_rows = jnp.einsum(
            "hqk,khe->qhe", attn_probs, values_all, preferred_element_type=jnp.float32
        )
        log_total = (largest + jnp.log(totals))[..., 0]
        return (mixed_rows.astype(jnp.bfloat16), jnp.transpose(log_total))

    blocked = queries.reshape(block_count, block_rows, heads_here, HEAD_DIM)
    starts = jnp.arange(block_count, dtype=jnp.int32) * block_rows
    mixed_rows, log_total = lax.map(one_block, (blocked, starts))
    return (
        mixed_rows.reshape(length, 1, heads_here, HEAD_DIM),
        log_total.reshape(length, 1, heads_here),
        received,
    )


def attend_back(received, log_sum, grad_in):
    packed = received[:, 0]
    length = packed.shape[0]
    heads_here = packed.shape[1]
    queries = packed[..., :HEAD_DIM]
    keys_all = packed[..., HEAD_DIM : 2 * HEAD_DIM]
    values_all = packed[..., 2 * HEAD_DIM :]
    block_rows = min(512, length)
    block_count = length // block_rows
    score_scale = HEAD_DIM ** (-0.5)

    def one_block(running, element):
        key_acc, value_acc = running
        query_rows, grad_rows, log_rows, row_start = element
        scores = (
            jnp.einsum("qhe,khe->hqk", query_rows, keys_all, preferred_element_type=jnp.float32)
            * score_scale
        )
        scores = jnp.where(block_mask(row_start, block_rows, length)[None], scores, -1e30)
        attn_probs = jnp.exp(scores - jnp.transpose(log_rows)[:, :, None])
        value_acc = value_acc + jnp.einsum(
            "hqk,qhe->khe",
            attn_probs.astype(jnp.bfloat16),
            grad_rows,
            preferred_element_type=jnp.float32,
        )
        grad_probs = jnp.einsum(
            "qhe,khe->hqk", grad_rows, values_all, preferred_element_type=jnp.float32
        )
        centre = jnp.sum(attn_probs * grad_probs, axis=-1, keepdims=True)
        grad_scores = (attn_probs * (grad_probs - centre)).astype(jnp.bfloat16)
        query_grad = (
            jnp.einsum("hqk,khe->qhe", grad_scores, keys_all, preferred_element_type=jnp.float32)
            * score_scale
        )
        key_acc = key_acc + jnp.einsum(
            "hqk,qhe->khe", grad_scores, query_rows, preferred_element_type=jnp.float32
        )
        return ((key_acc, value_acc), query_grad)

    empty_acc = jnp.zeros((length, heads_here, HEAD_DIM), jnp.float32)
    blocked_query = queries.reshape(block_count, block_rows, heads_here, HEAD_DIM)
    blocked_grad = grad_in[:, 0].reshape(block_count, block_rows, heads_here, HEAD_DIM)
    blocked_log = log_sum[:, 0].reshape(block_count, block_rows, heads_here)
    starts = jnp.arange(block_count, dtype=jnp.int32) * block_rows
    (key_acc, value_acc), query_grads = lax.scan(
        one_block, (empty_acc, empty_acc), (blocked_query, blocked_grad, blocked_log, starts)
    )
    stacked = jnp.stack(
        [query_grads.reshape(length, heads_here, HEAD_DIM), key_acc * score_scale, value_acc],
        axis=2,
    )
    return stacked.astype(jnp.bfloat16).reshape(length, 1, heads_here, 3 * HEAD_DIM)


def norm_back(values, scale_rows, gain_row, upstream):
    scaled = upstream * gain_row
    gain_term = jnp.sum(upstream * values * scale_rows, axis=0)
    value_grad = scale_rows * scaled - values * scale_rows**3 * jnp.mean(
        scaled * values, axis=-1, keepdims=True
    )
    return (gain_term, value_grad)


def on_device(
    inputs,
    attn_gain,
    qkv_weight,
    out_weight,
    ffn_gain,
    router_weight,
    expert_in,
    expert_out,
    shared_in,
    shared_out,
    routes,
    slot_index,
    cotangent,
):
    tok_rows = inputs.shape[1]
    group_count = lax.axis_size("seq")
    heads_group = HEADS // group_count
    stream = inputs[0].astype(jnp.float32)
    attn_local = (
        attn_gain.astype(jnp.bfloat16),
        qkv_weight.astype(jnp.bfloat16),
        out_weight.astype(jnp.bfloat16),
    )
    attn_full = (
        lax.all_gather(attn_local[0], "dp", axis=0, tiled=True),
        lax.all_gather(attn_local[1], "dp", axis=0, tiled=True),
        lax.all_gather(attn_local[2], "dp", axis=0, tiled=True),
    )
    gain_first, qkv_full, out_full = attn_full
    positions = lax.axis_index("seq") * tok_rows + jnp.arange(tok_rows, dtype=jnp.int32)
    cos_table, sine_table = rotary_tables(positions)
    scale_one = lax.rsqrt(jnp.mean(stream * stream, axis=-1, keepdims=True) + EPSILON)
    gain_one_f = gain_first.astype(jnp.float32)
    normed = (stream * scale_one * gain_one_f).astype(jnp.bfloat16)
    projected = jnp.einsum("td,dhce->thce", normed, qkv_full, preferred_element_type=jnp.float32)
    rotated = jnp.stack(
        [
            rotate(projected[:, :, 0], cos_table, sine_table),
            rotate(projected[:, :, 1], cos_table, sine_table),
            projected[:, :, 2],
        ],
        axis=2,
    ).astype(jnp.bfloat16)
    outgoing = rotated.reshape(tok_rows, group_count, heads_group, 3 * HEAD_DIM)
    head_out, log_sum, head_qkv = attend_heads(
        lax.all_to_all(outgoing, "seq", split_axis=1, concat_axis=0, tiled=True)
    )
    attended = lax.all_to_all(head_out, "seq", split_axis=0, concat_axis=1, tiled=True).reshape(
        tok_rows, D
    )
    middle = stream + jnp.dot(attended, out_full, preferred_element_type=jnp.float32)
    ffn_local = (
        ffn_gain.astype(jnp.bfloat16),
        router_weight.astype(jnp.bfloat16),
        expert_in.astype(jnp.bfloat16),
        expert_out.astype(jnp.bfloat16),
        shared_in.astype(jnp.bfloat16),
        shared_out.astype(jnp.bfloat16),
    )
    ffn_full = (
        lax.all_gather(ffn_local[0], "dp", axis=0, tiled=True),
        lax.all_gather(ffn_local[1], "dp", axis=0, tiled=True),
        lax.all_gather(ffn_local[2], "dp", axis=1, tiled=True),
        lax.all_gather(ffn_local[3], "dp", axis=1, tiled=True),
        lax.all_gather(ffn_local[4], "dp", axis=0, tiled=True),
        lax.all_gather(ffn_local[5], "dp", axis=0, tiled=True),
    )
    gain_second, router_full, exp_in_full, exp_out_full, sh_in_full, sh_out_full = ffn_full
    scale_two = lax.rsqrt(jnp.mean(middle * middle, axis=-1, keepdims=True) + EPSILON)
    gain_two_f = gain_second.astype(jnp.float32)
    normed_two = (middle * scale_two * gain_two_f).astype(jnp.bfloat16)
    logits = jnp.dot(normed_two, router_full, preferred_element_type=jnp.float32)
    router_probs = jax.nn.softmax(logits, axis=-1)
    route_rows = routes[0]
    choice_hot = (
        route_rows[:, :, None] == jnp.arange(EXPERTS, dtype=jnp.int32)[None, None, :]
    ).astype(jnp.float32)
    gate_values = jnp.sum(choice_hot * router_probs[:, None, :], axis=-1)
    flat_slot = (route_rows * CAP + slot_index[0]).reshape(-1)
    buffer = (
        jnp.zeros((EXPERTS * CAP, D), jnp.bfloat16)
        .at[flat_slot]
        .set(jnp.repeat(normed_two, TOP, axis=0))
        .reshape(EXPERTS, CAP, D)
    )
    gate_up = jnp.einsum("ecd,edf->ecf", buffer, exp_in_full, preferred_element_type=jnp.float32)
    activated = (jax.nn.silu(gate_up[..., :FF]) * gate_up[..., FF:]).astype(jnp.bfloat16)
    expert_rows = jnp.einsum(
        "ecf,efd->ecd", activated, exp_out_full, preferred_element_type=jnp.float32
    ).reshape(EXPERTS * CAP, D)
    picked = expert_rows[flat_slot].reshape(tok_rows, TOP, D)
    mixture = jnp.sum(gate_values[:, :, None] * picked, axis=1)
    shared_gu = jnp.dot(normed_two, sh_in_full, preferred_element_type=jnp.float32)
    shared_act = (jax.nn.silu(shared_gu[:, :FF]) * shared_gu[:, FF:]).astype(jnp.bfloat16)
    result = middle + mixture + jnp.dot(shared_act, sh_out_full, preferred_element_type=jnp.float32)
    output = result.astype(jnp.bfloat16)[None]
    ffn_back = (
        lax.all_gather(ffn_local[0], "dp", axis=0, tiled=True),
        lax.all_gather(ffn_local[1], "dp", axis=0, tiled=True),
        lax.all_gather(ffn_local[2], "dp", axis=1, tiled=True),
        lax.all_gather(ffn_local[3], "dp", axis=1, tiled=True),
        lax.all_gather(ffn_local[4], "dp", axis=0, tiled=True),
        lax.all_gather(ffn_local[5], "dp", axis=0, tiled=True),
    )
    router_back, exp_in_back, exp_out_back, sh_in_back, sh_out_back = (
        ffn_back[1],
        ffn_back[2],
        ffn_back[3],
        ffn_back[4],
        ffn_back[5],
    )
    upstream = cotangent[0].astype(jnp.float32)
    grad_low = upstream.astype(jnp.bfloat16)
    shared_out_grad = jnp.einsum(
        "tf,td->fd", shared_act, grad_low, preferred_element_type=jnp.float32
    )
    shared_act_grad = jnp.einsum(
        "td,fd->tf", grad_low, sh_out_back, preferred_element_type=jnp.float32
    )
    shared_gu_grad = silu_grads(shared_gu[:, :FF], shared_gu[:, FF:], shared_act_grad).astype(
        jnp.bfloat16
    )
    shared_in_grad = jnp.einsum(
        "td,tf->df", normed_two, shared_gu_grad, preferred_element_type=jnp.float32
    )
    norm_grad_two = jnp.einsum(
        "tf,df->td", shared_gu_grad, sh_in_back, preferred_element_type=jnp.float32
    )
    slot_terms = (gate_values[:, :, None] * upstream[:, None, :]).reshape(tok_rows * TOP, D)
    slot_grad = (
        jnp.zeros((EXPERTS * CAP, D), jnp.float32)
        .at[flat_slot]
        .set(slot_terms)
        .astype(jnp.bfloat16)
        .reshape(EXPERTS, CAP, D)
    )
    expert_out_grad = jnp.einsum(
        "ecf,ecd->efd", activated, slot_grad, preferred_element_type=jnp.float32
    )
    activated_grad = jnp.einsum(
        "ecd,efd->ecf", slot_grad, exp_out_back, preferred_element_type=jnp.float32
    )
    gate_up_grad = silu_grads(gate_up[..., :FF], gate_up[..., FF:], activated_grad).astype(
        jnp.bfloat16
    )
    expert_in_grad = jnp.einsum(
        "ecd,ecf->edf", buffer, gate_up_grad, preferred_element_type=jnp.float32
    )
    buffer_grad = jnp.einsum(
        "ecf,edf->ecd", gate_up_grad, exp_in_back, preferred_element_type=jnp.float32
    ).reshape(EXPERTS * CAP, D)
    norm_grad_two = norm_grad_two + jnp.sum(
        buffer_grad[flat_slot].reshape(tok_rows, TOP, D), axis=1
    )
    gate_grad = jnp.sum(upstream[:, None, :] * picked, axis=-1)
    prob_grad = jnp.sum(choice_hot * gate_grad[:, :, None], axis=1)
    logit_grad = (
        router_probs * (prob_grad - jnp.sum(router_probs * prob_grad, axis=-1, keepdims=True))
    ).astype(jnp.bfloat16)
    router_weight_grad = jnp.einsum(
        "td,te->de", normed_two, logit_grad, preferred_element_type=jnp.float32
    )
    norm_grad_two = norm_grad_two + jnp.einsum(
        "te,de->td", logit_grad, router_back, preferred_element_type=jnp.float32
    )
    ffn_gain_term, middle_part = norm_back(middle, scale_two, gain_two_f, norm_grad_two)
    middle_grad = upstream + middle_part
    attn_back = (
        lax.all_gather(attn_local[0], "dp", axis=0, tiled=True),
        lax.all_gather(attn_local[1], "dp", axis=0, tiled=True),
        lax.all_gather(attn_local[2], "dp", axis=0, tiled=True),
    )
    qkv_back, out_back = (attn_back[1], attn_back[2])
    middle_low = middle_grad.astype(jnp.bfloat16)
    out_weight_grad = jnp.einsum(
        "tf,td->fd", attended, middle_low, preferred_element_type=jnp.float32
    )
    attended_grad = jnp.einsum(
        "td,fd->tf", middle_low, out_back, preferred_element_type=jnp.float32
    ).astype(jnp.bfloat16)
    head_grad = lax.all_to_all(
        attended_grad.reshape(tok_rows, group_count, heads_group, HEAD_DIM),
        "seq",
        split_axis=1,
        concat_axis=0,
        tiled=True,
    )
    stacked = attend_back(head_qkv, log_sum, head_grad)
    returned = (
        lax.all_to_all(stacked, "seq", split_axis=0, concat_axis=1, tiled=True)
        .reshape(tok_rows, HEADS, 3, HEAD_DIM)
        .astype(jnp.float32)
    )
    projected_grad = jnp.stack(
        [
            unrotate(returned[:, :, 0], cos_table, sine_table),
            unrotate(returned[:, :, 1], cos_table, sine_table),
            returned[:, :, 2],
        ],
        axis=2,
    ).astype(jnp.bfloat16)
    qkv_weight_grad = jnp.einsum(
        "td,thce->dhce", normed, projected_grad, preferred_element_type=jnp.float32
    )
    norm_grad = jnp.einsum(
        "thce,dhce->td", projected_grad, qkv_back, preferred_element_type=jnp.float32
    )
    attn_gain_term, input_part = norm_back(stream, scale_one, gain_one_f, norm_grad)
    input_grad = (middle_grad + input_part)[None]
    parts = (
        lax.psum_scatter(
            qkv_weight_grad.astype(jnp.bfloat16), "seq", scatter_dimension=1, tiled=True
        ).astype(jnp.float32),
        lax.psum_scatter(
            out_weight_grad.astype(jnp.bfloat16), "seq", scatter_dimension=1, tiled=True
        ).astype(jnp.float32),
        lax.psum_scatter(
            expert_in_grad.astype(jnp.bfloat16), "seq", scatter_dimension=2, tiled=True
        ).astype(jnp.float32),
        lax.psum_scatter(
            expert_out_grad.astype(jnp.bfloat16), "seq", scatter_dimension=2, tiled=True
        ).astype(jnp.float32),
        lax.psum_scatter(
            shared_in_grad.astype(jnp.bfloat16), "seq", scatter_dimension=1, tiled=True
        ).astype(jnp.float32),
        lax.psum_scatter(
            shared_out_grad.astype(jnp.bfloat16), "seq", scatter_dimension=1, tiled=True
        ).astype(jnp.float32),
    )
    owned = (
        lax.psum_scatter(attn_gain_term, "dp", scatter_dimension=0, tiled=True),
        lax.psum_scatter(ffn_gain_term, "dp", scatter_dimension=0, tiled=True),
        lax.psum_scatter(router_weight_grad, "dp", scatter_dimension=0, tiled=True),
        lax.psum_scatter(parts[0], "dp", scatter_dimension=0, tiled=True),
        lax.psum_scatter(parts[1], "dp", scatter_dimension=0, tiled=True),
        lax.psum_scatter(parts[2], "dp", scatter_dimension=1, tiled=True),
        lax.psum_scatter(parts[3], "dp", scatter_dimension=1, tiled=True),
        lax.psum_scatter(parts[4], "dp", scatter_dimension=0, tiled=True),
        lax.psum_scatter(parts[5], "dp", scatter_dimension=0, tiled=True),
    )
    small = lax.psum((owned[0], owned[1], owned[2]), "seq")
    joined = (
        lax.all_gather(owned[3].astype(jnp.bfloat16), "seq", axis=1, tiled=True).astype(
            jnp.float32
        ),
        lax.all_gather(owned[4].astype(jnp.bfloat16), "seq", axis=1, tiled=True).astype(
            jnp.float32
        ),
        lax.all_gather(owned[5].astype(jnp.bfloat16), "seq", axis=2, tiled=True).astype(
            jnp.float32
        ),
        lax.all_gather(owned[6].astype(jnp.bfloat16), "seq", axis=2, tiled=True).astype(
            jnp.float32
        ),
        lax.all_gather(owned[7].astype(jnp.bfloat16), "seq", axis=1, tiled=True).astype(
            jnp.float32
        ),
        lax.all_gather(owned[8].astype(jnp.bfloat16), "seq", axis=1, tiled=True).astype(
            jnp.float32
        ),
    )
    return (
        output,
        input_grad,
        small[0],
        joined[0],
        joined[1],
        small[1],
        small[2],
        joined[2],
        joined[3],
        joined[4],
        joined[5],
    )


def solution(mesh):
    return jax.shard_map(
        on_device,
        mesh=mesh,
        in_specs=(
            P("dp", "seq", None),
            P("dp"),
            P("dp", None, None, None),
            P("dp", None),
            P("dp"),
            P("dp", None),
            P(None, "dp", None),
            P(None, "dp", None),
            P("dp", None),
            P("dp", None),
            P("dp", "seq", None),
            P("dp", "seq", None),
            P("dp", "seq", None),
        ),
        out_specs=(
            P("dp", "seq", None),
            P("dp", "seq", None),
            P("dp"),
            P("dp", None, None, None),
            P("dp", None),
            P("dp"),
            P("dp", None),
            P(None, "dp", None),
            P(None, "dp", None),
            P("dp", None),
            P("dp", None),
        ),
        check_vma=False,
    )
```

profile of v0, /device:TPU:0, one launch (start us, length us, event | category | flops | bytes accessed | tf_op | source)
XLA Modules:
  0.0 1840.2 jit_solution(10139668922806943971)
XLA Ops:
  11.2 4.1 convert_element_type.229
  22.5 24.5 %all-reduce.6 = (bf16[768]{0:T(1024)(128)(2,1)S(1)}, bf16[768]{0:T(1024)(128)(2,1)}) all-reduce(bf16[768]{0:T(1024)(128)(2,1)S(1)} %dynamic-update-slice, bf16[768]{0:T(1024)(128)(2,1)S(1)} %dynamic-update-slice.1), channel_id=1, replica_groups=mesh['dp'=8,'seq'=4] {'dp'}, use_global_device_ids=true, to_apply=%add | all-reduce | flops 1536 | bytes 6144
  47.9 103.9 %all-gather.10.cloned.1.call-done = bf16[768,12,3,64]{3,1,2,0:T(8,128)(2,1)} async-done(((bf16[96,12,3,64]{3,1,2,0:T(8,128)(2,1)}), bf16[768,12,3,64]{3,1,2,0:T(8,128)(2,1)}) %all-gather.10.cloned.1.call-update) | async-done | bytes 3538960 | tf_op jit(solution)/shard_map/all_gather | solution.py:197
  151.8 10.9 copy.182
  162.7 3.2 fusion.89
  167.6 3.7 all-to-all-start
  172.8 14.3 all-to-all-done
  193.3 20.7 %while.33 = (s32[]{:T(128)}, bf16[2,512,3,64]{1,3,2,0:T(8,128)(2,1)}, f32[2,512,3]{1,2,0:T(4,128)}, s32[2]{0:T(128)}, bf16[2,512,3,64]{1,3,2,0:T(8,128)(2,1)}, /...) while((s32[]{:T(128)}, bf16[2,512,3,64]{1,3,2,0:T(8,128)(2,1)}, ...), condition=%wide.region_4.5_spmd, body=%wide.region_1.4_spmd.sunk | while | flops 422164992 | bytes 25364656 | solution.py:99
  199.7 3.2 fusion.167
  210.1 3.2 fusion.167
  217.1 4.1 all-to-all-start.1
  224.6 17.8 all-gather
  249.3 4.6 scatter_custom_fusion.1
  256.4 3.7 scatter_custom_fusion
  260.1 297.3 %all-gather.14.cloned.1.call-done = bf16[3,768,4096]{2,1,0:T(8,128)(2,1)} async-done(((bf16[3,96,4096]{2,1,0:T(8,128)(2,1)}), bf16[3,768,4096]{2,1,0:T(8,128)(2,1)}) %all-gather.14.cloned.1.call-update) | async-done | bytes 18874384 | tf_op jit(solution)/shard_map/all_gather | solution.py:234
  557.4 13.9 fusion.100
  571.3 126.2 %all-gather.16.cloned.1.call-done = bf16[3,2048,768]{2,1,0:T(8,128)(2,1)} async-done(((bf16[3,256,768]{2,1,0:T(8,128)(2,1)}), bf16[3,2048,768]{2,1,0:T(8,128)(2,1)}) %all-gather.16.cloned.1.call-update) | async-done | bytes 9437200 | tf_op jit(solution)/shard_map/all_gather | solution.py:235
  697.5 10.2 multiply_convert_fusion.2
  709.3 5.1 convolution_convert_fusion.2
  714.5 11.6 convolution_convert_fusion
  726.5 70.9 %all-gather.18.cloned.1.call-done = bf16[768,4096]{1,0:T(8,128)(2,1)} async-done(((bf16[96,4096]{1,0:T(8,128)(2,1)}), bf16[768,4096]{1,0:T(8,128)(2,1)}) %all-gather.18.cloned.1.call-update) | async-done | bytes 6291472 | tf_op jit(solution)/shard_map/all_gather | solution.py:236
  797.4 6.6 fusion.102
  803.9 54.1 %all-gather.20.cloned.1.call-done = bf16[2048,768]{1,0:T(8,128)(2,1)} async-done(((bf16[256,768]{1,0:T(8,128)(2,1)}), bf16[2048,768]{1,0:T(8,128)(2,1)}) %all-gather.20.cloned.1.call-update) | async-done | bytes 3145744 | tf_op jit(solution)/shard_map/all_gather | solution.py:237
  858.1 6.0 multiply_convert_fusion.5
  868.1 7.1 convolution_convert_fusion.1
  875.2 6.6 fusion.101
  887.6 11.6 fusion.56
  901.7 3.1 reshape.378
  904.8 3.3 reduce_sum.148
  908.1 5.0 multiply_reduce_fusion.1
  913.3 5.3 fusion.64
  921.4 3.7 all-to-all-start.2
  925.1 11.9 all-to-all-done.2
  938.4 42.2 %while.34 = (s32[]{:T(128)}, f32[1024,3,64]{0,2,1:T(8,128)}, f32[1024,3,64]{0,2,1:T(8,128)}, bf16[2,512,3,64]{1,3,2,0:T(8,128)(2,1)}, bf16[2,512,3,64]{1,3,2,0:T...) while((s32[]{:T(128)}, f32[1024,3,64]{0,2,1:T(8,128)}, ...), condition=%wide.region_19.20_spmd.clone, body=%wide.region_17.19_spmd.clone.sunk | while | flops 1031649792 | bytes 110418240 | solution.py:152
  943.9 3.8 multiply_reduce_fusion.8
  953.3 4.2 fusion.179
  965.0 4.1 multiply_reduce_fusion.8
  974.5 4.3 fusion.179
  986.4 4.6 all-to-all-start.3
  992.6 46.9 %all-to-all-done.3 = bf16[1024,1,3,192]{3,2,1,0:T(4,128)(2,1)} async-done(((bf16[1024,1,3,192]{3,2,1,0:T(4,128)(2,1)}), bf16[1024,1,3,192]{3,2,1,0:T(4,128)(2,1)}, u32[]{:S(2)}, u32[]{:S(2)}) %all-to-all-start.3) | async-done | bytes 1179680 | tf_op jit(solution)/shard_map/all_to_all | solution.py:361
  1039.5 4.1 copy.216
  1051.5 55.1 %reduce-scatter.24.cloned.1.call-done = bf16[3,768,1024]{2,1,0:T(8,128)(2,1)} async-done(((bf16[3,768,4096]{2,1,0:T(8,128)(2,1)}), bf16[3,768,1024]{2,1,0:T(8,128)(2,1)}) %reduce-scatter.24.cloned.1.call-update) | async-done | bytes 4718608 | tf_op jit(solution)/shard_map/reduce_scatter | solution.py:388
  1106.7 40.6 %reduce-scatter.36.cloned.1.call-done = bf16[2048,192]{0,1:T(8,128)(2,1)} async-done(((bf16[2048,768]{0,1:T(8,128)(2,1)}), bf16[2048,192]{0,1:T(8,128)(2,1)}) %reduce-scatter.36.cloned.1.call-update) | async-done | bytes 786448 | tf_op jit(solution)/shard_map/reduce_scatter | solution.py:397
  1147.3 60.7 %reduce-scatter.32.cloned.1.call-done = bf16[768,1024]{1,0:T(8,128)(2,1)} async-done(((bf16[768,4096]{1,0:T(8,128)(2,1)}), bf16[768,1024]{1,0:T(8,128)(2,1)}) %reduce-scatter.32.cloned.1.call-update) | async-done | bytes 1572880 | tf_op jit(solution)/shard_map/reduce_scatter | solution.py:394
  1209.3 27.8 %reduce-scatter.22.cloned.1.call-done = bf16[768,192]{0,1:T(8,128)(2,1)} async-done(((bf16[768,768]{0,1:T(8,128)(2,1)}), bf16[768,192]{0,1:T(8,128)(2,1)}) %reduce-scatter.22.cloned.1.call-update) | async-done | bytes 294928 | tf_op jit(solution)/shard_map/reduce_scatter | solution.py:385
  1239.3 41.3 %reduce-scatter.20.cloned.1.call-done = bf16[768,3,3,64]{0,3,2,1:T(8,128)(2,1)} async-done(((bf16[768,12,3,64]{0,3,2,1:T(8,128)(2,1)}), bf16[768,3,3,64]{0,3,2,1:T(8,128)(2,1)}) %reduce-scatter.20.cloned.1.call-update) | async-done | bytes 884752 | tf_op jit(solution)/shard_map/reduce_scatter | solution.py:382
  1283.7 70.4 %reduce-scatter.30.cloned.1.call-done = bf16[3,256,192]{1,2,0:T(8,128)(2,1)} async-done(((bf16[3,2048,192]{1,2,0:T(8,128)(2,1)}), bf16[3,256,192]{1,2,0:T(8,128)(2,1)}) %reduce-scatter.30.cloned.1.call-update) | async-done | bytes 294928 | tf_op jit(solution)/shard_map/reduce_scatter | solution.py:408
  1354.1 98.4 %reduce-scatter.26.cloned.1.call-done = bf16[3,96,1024]{2,1,0:T(8,128)(2,1)} async-done(((bf16[3,768,1024]{2,1,0:T(8,128)(2,1)}), bf16[3,96,1024]{2,1,0:T(8,128)(2,1)}) %reduce-scatter.26.cloned.1.call-update) | async-done | bytes 589840 | tf_op jit(solution)/shard_map/reduce_scatter | solution.py:407
  1453.1 65.9 %reduce-scatter.38.cloned.1.call-done = bf16[256,192]{0,1:T(8,128)(2,1)} async-done(((bf16[2048,192]{0,1:T(8,128)(2,1)}), bf16[256,192]{0,1:T(8,128)(2,1)}) %reduce-scatter.38.cloned.1.call-update) | async-done | bytes 98320 | tf_op jit(solution)/shard_map/reduce_scatter | solution.py:410
  1519.0 6.6 all_gather.66
  1526.6 59.5 %reduce-scatter.34.cloned.1.call-done = bf16[96,1024]{1,0:T(8,128)(2,1)} async-done(((bf16[768,1024]{1,0:T(8,128)(2,1)}), bf16[96,1024]{1,0:T(8,128)(2,1)}) %reduce-scatter.34.cloned.1.call-update) | async-done | bytes 196624 | tf_op jit(solution)/shard_map/reduce_scatter | solution.py:409
  1586.2 8.9 all_gather.65
  1596.4 3.4 fusion.66
  1599.7 50.2 %reduce-scatter.44.cloned.1.call-done = f32[96,3]{1,0:T(8,128)} async-done(((f32[768,3]{1,0:T(8,128)}), f32[96,3]{1,0:T(8,128)}) %reduce-scatter.44.cloned.1.call-update) | async-done | bytes 1168
  1650.8 6.7 fusion.77
  1657.5 19.9 %all-reduce.4 = (f32[768]{0:T(1024)S(1)}, f32[768]{0:T(1024)S(1)}) all-reduce(f32[768]{0:T(1024)} %get-tuple-element.501, f32[768]{0:T(1024)S(1)} %copy-done.46), channel_id=2, replica_groups=mesh['dp'=8,'seq'=4] {'dp'}, use_global_device_ids=true, to_apply=%region_22.23.clone | all-reduce | flops 1536 | bytes 12288
  1677.5 6.5 all-reduce.5
  1686.5 28.5 %reduce-scatter.42.cloned.1.call-done = f32[96,192]{1,0:T(8,128)} async-done(((f32[768,192]{1,0:T(8,128)}), f32[96,192]{1,0:T(8,128)}) %reduce-scatter.42.cloned.1.call-update) | async-done | bytes 73744
  1716.0 5.6 all_gather.62
  1722.5 62.3 %reduce-scatter.40.cloned.1.call-done = f32[96,576]{1,0:T(8,128)} async-done(((f32[768,576]{1,0:T(8,128)}), f32[96,576]{1,0:T(8,128)}) %reduce-scatter.40.cloned.1.call-update) | async-done | bytes 221200
  1785.9 7.5 all_gather.61
  1794.6 8.1 all-gather.24.cloned.1.call-done
  1805.4 23.0 %all-gather.22.cloned.1.call-done = bf16[3,96,4096]{2,1,0:T(8,128)(2,1)} async-done(((bf16[3,96,1024]{2,1,0:T(8,128)(2,1)}), bf16[3,96,4096]{2,1,0:T(8,128)(2,1)}) %all-gather.22.cloned.1.call-update) | async-done | bytes 2359312 | tf_op jit(solution)/shard_map/all_gather | solution.py:420
  1828.5 4.4 convert_element_type.257
  (321 shorter events, 129.1 us)
Async XLA Ops:
  7.2 144.6 %all-gather.10.cloned.1.call-start = ((), (), s32[]{:S(2)}) async-start(), calls=%async_computation.17 | async-start | bytes 10616832 | tf_op jit(solution)/shard_map/all_gather | solution.py:197
  10.4 234.5 %all-gather.12.cloned.1.call-start = ((), (), s32[]{:S(2)}) async-start(), calls=%async_computation.18 | async-start | bytes 1327104 | tf_op jit(solution)/shard_map/all_gather | solution.py:198
  11.2 546.2 %all-gather.14.cloned.1.call-start = ((), (), s32[]{:S(2)}) async-start(), calls=%async_computation.19 | async-start | bytes 21233664 | tf_op jit(solution)/shard_map/all_gather | solution.py:234
  15.3 682.2 %all-gather.16.cloned.1.call-start = ((), (), s32[]{:S(2)}) async-start(), calls=%async_computation.20 | async-start | bytes 10616832 | tf_op jit(solution)/shard_map/all_gather | solution.py:235
  18.2 28.9 %copy-start.15 = (bf16[1,256,768]{2,1,0:T(8,128)(2,1)S(1)}, bf16[1,256,768]{2,1,0:T(8,128)(2,1)}, u32[]{:S(2)}) copy-start(bf16[1,256,768]{2,1,0:T(8,128)(2,1)} %param.17) | copy-start | bytes 1179652
  18.2 779.2 %all-gather.18.cloned.1.call-start = ((), (), s32[]{:S(2)}) async-start(), calls=%async_computation.21 | async-start | bytes 7077888 | tf_op jit(solution)/shard_map/all_gather | solution.py:236
  47.0 115.7 %copy-start.40 = (f32[768]{0:T(1024)}, f32[768]{0:T(1024)S(1)}, u32[]{:S(2)}) copy-start(f32[768]{0:T(1024)S(1)} %convert_element_type.219) | copy-start | bytes 9220
  47.7 115.0 %copy-start.49 = (f32[256]{0:T(256)}, f32[256]{0:T(256)S(1)}, u32[]{:S(2)}) copy-start(f32[256]{0:T(256)S(1)} %get-tuple-element.576) | copy-start | bytes 3076
  47.9 118.2 %copy-start.33 = (f32[256,32]{0,1:T(8,128)}, f32[256,32]{0,1:T(8,128)S(1)}, u32[]{:S(2)}) copy-start(f32[256,32]{0,1:T(8,128)S(1)} %get-tuple-element.573) | copy-start | bytes 98308
  47.9 118.2 %copy-start.35 = (f32[256,32]{0,1:T(8,128)}, f32[256,32]{0,1:T(8,128)S(1)}, u32[]{:S(2)}) copy-start(f32[256,32]{0,1:T(8,128)S(1)} %get-tuple-element.574) | copy-start | bytes 98308
  166.5 4.9 copy-start.28
  167.6 5.1 copy-start.44
  167.6 5.1 copy-start.52
  167.6 5.1 copy-start.20
  167.6 19.5 %all-to-all-start = ((bf16[256,4,3,192]{0,3,2,1:T(8,128)(2,1)}), bf16[256,4,3,192]{0,3,2,1:T(8,128)(2,1)S(1)}, u32[]{:S(2)}, u32[]{:S(2)}) async-start(bf16[256,4,3,192]{0,3,2,1:T(8,128)(2,1)} %bitcast.16), calls=%async_computation | async-start | bytes 2359296 | tf_op jit(solution)/shard_map/all_to_all | solution.py:217
  171.3 686.8 %all-gather.20.cloned.1.call-start = ((), (), s32[]{:S(2)}) async-start(), calls=%async_computation.22 | async-start | bytes 3538944 | tf_op jit(solution)/shard_map/all_gather | solution.py:237
  172.8 49.0 %copy-start.11 = (f32[256,768]{1,0:T(8,128)}, f32[256,768]{1,0:T(8,128)S(1)}, u32[]{:S(2)}) copy-start(f32[256,768]{1,0:T(8,128)S(1)} %bitcast_convert_fusion.1) | copy-start | bytes 2359300
  214.1 7.4 copy-start.55
  214.1 7.4 copy-start.53
  217.1 25.4 %all-to-all-start.1 = ((bf16[4,2,24576]{2,1,0:T(2,128)(2,1)}), bf16[4,2,24576]{2,1,0:T(2,128)(2,1)}, u32[]{:S(2)}, u32[]{:S(2)}) async-start(bf16[4,2,24576]{2,1,0:T(2,128)(2,1)} %reshape.442), calls=%async_computation.1 | async-start | bytes 786432 | tf_op jit(solution)/shard_map/all_to_all | solution.py:219
  221.2 829.5 %reduce-scatter.28.cloned.1.call-start = ((), (), s32[]{:S(2)}) async-start(), calls=%async_computation.28 | async-start | bytes 11796480 | tf_op jit(solution)/shard_map/reduce_scatter | solution.py:391
  246.9 672.8 %copy-start.7 = (f32[256,768]{1,0:T(8,128)}, f32[256,768]{1,0:T(8,128)S(1)}, u32[]{:S(2)}) copy-start(f32[256,768]{1,0:T(8,128)S(1)} %get-tuple-element.582) | copy-start | bytes 2359300
  247.1 621.1 %copy-start.4 = (bf16[256,768]{1,0:T(8,128)(2,1)}, bf16[256,768]{1,0:T(8,128)(2,1)S(1)}, u32[]{:S(2)}) copy-start(bf16[256,768]{1,0:T(8,128)(2,1)S(1)} %multiply_convert_fusion.8) | copy-start | bytes 1179652
  249.0 669.6 %copy-start.38 = (f32[256]{0:T(256)}, f32[256]{0:T(256)S(1)}, u32[]{:S(2)}) copy-start(f32[256]{0:T(256)S(1)} %get-tuple-element.583) | copy-start | bytes 3076
  249.0 669.6 %copy-start.42 = (f32[256]{0:T(256)}, f32[256]{0:T(256)S(1)}, u32[]{:S(2)}) copy-start(f32[256]{0:T(256)S(1)} %fusion.92) | copy-start | bytes 3076
  697.5 11.7 copy-start.18
  714.4 392.1 %reduce-scatter.24.cloned.1.call-start = ((), (), s32[]{:S(2)}) async-start(), calls=%async_computation.25 | async-start | bytes 23592960 | tf_op jit(solution)/shard_map/reduce_scatter | solution.py:388
  726.0 421.2 %reduce-scatter.36.cloned.1.call-start = ((), (), s32[]{:S(2)}) async-start(), calls=%async_computation.33 | async-start | bytes 3932160 | tf_op jit(solution)/shard_map/reduce_scatter | solution.py:397
  868.1 340.0 %reduce-scatter.32.cloned.1.call-start = ((), (), s32[]{:S(2)}) async-start(), calls=%async_computation.31 | async-start | bytes 7864320 | tf_op jit(solution)/shard_map/reduce_scatter | solution.py:394
  901.7 6.4 copy-start.12
  908.1 5.1 copy-start.45
  913.3 5.3 copy-start.47
  919.9 17.4 copy-start.9
  921.4 15.6 all-to-all-start.2
  940.3 7.4 copy-start
  953.3 4.2 copy-start.29
  961.3 7.7 copy-start
  965.0 4.1 copy-start.2
  974.5 4.3 copy-start.29
  986.4 4.7 copy-start.10
  986.4 4.7 copy-start.22
  986.4 53.2 %all-to-all-start.3 = ((bf16[1024,1,3,192]{3,2,1,0:T(4,128)(2,1)}), bf16[1024,1,3,192]{3,2,1,0:T(4,128)(2,1)}, u32[]{:S(2)}, u32[]{:S(2)}) async-start(bf16[1024,1,3,192]{3,2,1,0:T(4,128)(2,1)} %copy.203), calls=%async_computation.3 | async-start | bytes 4194304 | tf_op jit(solution)/shard_map/all_to_all | solution.py:361
  991.0 246.1 %reduce-scatter.22.cloned.1.call-start = ((), (), s32[]{:S(2)}) async-start(), calls=%async_computation.24 | async-start | bytes 1474560 | tf_op jit(solution)/shard_map/reduce_scatter | solution.py:385
  992.6 288.0 %reduce-scatter.20.cloned.1.call-start = ((), (), s32[]{:S(2)}) async-start(), calls=%async_computation.23 | async-start | bytes 4423680 | tf_op jit(solution)/shard_map/reduce_scatter | solution.py:382
  1050.7 303.4 %reduce-scatter.30.cloned.1.call-start = ((), (), s32[]{:S(2)}) async-start(), calls=%async_computation.29 | async-start | bytes 2654208 | tf_op jit(solution)/shard_map/reduce_scatter | solution.py:408
  1051.4 401.1 %reduce-scatter.26.cloned.1.call-start = ((), (), s32[]{:S(2)}) async-start(), calls=%async_computation.26 | async-start | bytes 5308416 | tf_op jit(solution)/shard_map/reduce_scatter | solution.py:407
  1106.6 101.6 %copy-start.5 = (bf16[256,768]{1,0:T(8,128)(2,1)S(1)}, bf16[256,768]{1,0:T(8,128)(2,1)}, u32[]{:S(2)}) copy-start(bf16[256,768]{1,0:T(8,128)(2,1)} %copy-done.4) | copy-start | bytes 1179652
  1106.6 101.6 %copy-start.39 = (f32[256]{0:T(256)S(1)}, f32[256]{0:T(256)}, u32[]{:S(2)}) copy-start(f32[256]{0:T(256)} %copy-done.38) | copy-start | bytes 3076
  1106.6 101.6 %copy-start.43 = (f32[256]{0:T(256)S(1)}, f32[256]{0:T(256)}, u32[]{:S(2)}) copy-start(f32[256]{0:T(256)} %copy-done.42) | copy-start | bytes 3076
  1106.6 101.6 %copy-start.48 = (f32[256]{0:T(256)S(1)}, f32[256]{0:T(256)}, u32[]{:S(2)}) copy-start(f32[256]{0:T(256)} %copy-done.47) | copy-start | bytes 3076
  1106.6 412.3 %reduce-scatter.38.cloned.1.call-start = ((), (), s32[]{:S(2)}) async-start(), calls=%async_computation.34 | async-start | bytes 884736 | tf_op jit(solution)/shard_map/reduce_scatter | solution.py:410
  1147.3 438.9 %reduce-scatter.34.cloned.1.call-start = ((), (), s32[]{:S(2)}) async-start(), calls=%async_computation.32 | async-start | bytes 1769472 | tf_op jit(solution)/shard_map/reduce_scatter | solution.py:409
  1208.1 441.8 %reduce-scatter.44.cloned.1.call-start = ((), (), s32[]{:S(2)}) async-start(), calls=%async_computation.37 | async-start | bytes 442368
  1209.2 505.8 %reduce-scatter.42.cloned.1.call-start = ((), (), s32[]{:S(2)}) async-start(), calls=%async_computation.36 | async-start | bytes 884736
  1239.2 545.6 %reduce-scatter.40.cloned.1.call-start = ((), (), s32[]{:S(2)}) async-start(), calls=%async_computation.35 | async-start | bytes 2211840
  1283.7 519.0 %all-gather.24.cloned.1.call-start = ((), (), s32[]{:S(2)}) async-start(), calls=%async_computation.30 | async-start | bytes 1474560 | tf_op jit(solution)/shard_map/all_gather | solution.py:423
  1354.1 474.4 %all-gather.22.cloned.1.call-start = ((), (), s32[]{:S(2)}) async-start(), calls=%async_computation.27 | async-start | bytes 2949120 | tf_op jit(solution)/shard_map/all_gather | solution.py:420
  1525.6 70.7 %copy-start.8 = (f32[256,768]{1,0:T(8,128)S(1)}, f32[256,768]{1,0:T(8,128)}, u32[]{:S(2)}) copy-start(f32[256,768]{1,0:T(8,128)} %copy-done.7) | copy-start | bytes 2359300
  1586.2 10.2 copy-start.56
  1596.3 54.5 %copy-start.14 = (bf16[256,4,1,3,192]{0,4,3,2,1:T(8,128)(2,1)S(1)}, bf16[256,4,1,3,192]{0,4,3,2,1:T(8,128)(2,1)}, u32[]{:S(2)}) copy-start(bf16[256,4,1,3,192]{0,4,3,2,1:T(8,128)(2,1)} %copy-done.13) | copy-start | bytes 3538948
  1596.3 54.5 %copy-start.17 = (bf16[1,256,768]{2,1,0:T(8,128)(2,1)S(1)}, bf16[1,256,768]{2,1,0:T(8,128)(2,1)}, u32[]{:S(2)}) copy-start(bf16[1,256,768]{2,1,0:T(8,128)(2,1)} %param.17) | copy-start | bytes 1179652
  1596.3 54.5 %copy-start.26 = (bf16[256,12,1,64]{0,3,1,2:T(8,128)(2,1)S(1)}, bf16[256,12,1,64]{0,3,1,2:T(8,128)(2,1)}, u32[]{:S(2)}) copy-start(bf16[256,12,1,64]{0,3,1,2:T(8,128)(2,1)} %copy-done.25) | copy-start | bytes 1179652
  1596.3 54.5 %copy-start.51 = (f32[256]{0:T(256)S(1)}, f32[256]{0:T(256)}, u32[]{:S(2)}) copy-start(f32[256]{0:T(256)} %copy-done.49) | copy-start | bytes 3076
  1650.8 6.7 copy-start.46
  (27 other events, 47.6 us)
Sparse Core Ops, SparseCore 0:
  10.8 140.9 all-gather.9
  154.5 39.2 all-gather.11
  196.0 361.3 all-gather.13
  559.4 138.0 all-gather.15
  700.1 97.1 all-gather.17
  799.4 58.6 all-gather.19
  860.7 81.2 reduce-scatter.27
  944.6 161.9 reduce-scatter.23
  1109.2 37.9 reduce-scatter.35
  1149.6 58.3 reduce-scatter.31
  1211.4 25.7 reduce-scatter.21
  1240.1 40.4 reduce-scatter.19
  1284.5 69.5 reduce-scatter.29
  1358.0 94.4 reduce-scatter.25
  1456.0 62.8 reduce-scatter.37
  1522.2 63.8 reduce-scatter.33
  1589.6 60.2 reduce-scatter.43
  1653.4 61.5 reduce-scatter.41
  1719.1 65.7 reduce-scatter.39
  1786.3 16.3 all-gather.23
  1804.3 24.0 all-gather.21
where the time goes:
time: 1850 us; the launch traced here: 1840 us
  waiting for transfers between devices  1420 us (77%)
  matrix products  147 us (8%)
  blocking collectives  97.4 us (5%)
  local copies, waits for them, and re-layouts  85.9 us (5%)
  other arithmetic  56.9 us (3%)
    all_gather x1, waiting for transfers between devices, on_device(): lax.all_gather(ffn_local[2], 'dp', axis=1, tiled=True)  297 us
    unnamed x24, waiting for transfers between devices  142 us
    all_gather x1, waiting for transfers between devices, on_device(): lax.all_gather(ffn_local[3], 'dp', axis=1, tiled=True)  126 us
    all_gather x1, waiting for transfers between devices, on_device(): lax.all_gather(attn_local[1], 'dp', axis=0, tiled=True)  104 us
    reduce_scatter x1, waiting for transfers between devices, on_device(): lax.psum_scatter(parts[2], 'dp', scatter_dimension=1, tiled=True)  98.4 us
    all_gather x1, waiting for transfers between devices, on_device(): lax.all_gather(ffn_local[4], 'dp', axis=0, tiled=True)  70.9 us
    reduce_scatter x1, waiting for transfers between devices, on_device(): lax.psum_scatter(parts[3], 'dp', scatter_dimension=1, tiled=True)  70.4 us
    reduce_scatter x1, waiting for transfers between devices, on_device(): lax.psum_scatter(parts[5], 'dp', scatter_dimension=0, tiled=True)  65.9 us
  transfers between devices with their start and end apart: 25, of which 22 were waited for; matrix products, arithmetic and copies ran while one was open for 15% of the time, Pallas kernels for 0%

commit v1 on v0

--- a/solution.py
+++ b/solution.py
@@ -1,6 +1,12 @@
+import functools
+import types
+
 import jax
 import jax.numpy as jnp
+import numpy as np
 from jax import lax
+from jax.experimental import pallas as pl
+from jax.experimental.pallas import tpu as pltpu
 from jax.sharding import PartitionSpec as P
 
 D = 768
@@ -14,6 +20,7 @@
 
 
 EPSILON = 1e-05
+VMEM_LIMIT = 66_000_000
 
 
 def rotary_tables(positions):
@@ -445,9 +452,973 @@
     )
 
 
+MESH = pl.DeviceIdType.MESH
+BF = jnp.bfloat16
+F32 = jnp.float32
+TOK = ATT_BLOCK
+QKV_PAD = 640
+
+
+def nn(a, b):
+    return lax.dot_general(a, b, (((1,), (0,)), ((), ())), preferred_element_type=F32)
+
+
+def nt(a, b):
+    return lax.dot_general(a, b, (((1,), (1,)), ((), ())), preferred_element_type=F32)
+
+
+def tn(a, b):
+    return lax.dot_general(a, b, (((0,), (0,)), ((), ())), preferred_element_type=F32)
+
+
+def swap_halves(v):
+    lane = lax.broadcasted_iota(jnp.int32, v.shape, 1)
+    return jnp.where(lax.rem(lane, 64) < 32, pltpu.roll(v, 96, 1), pltpu.roll(v, 32, 1))
+
+
+def layer_kernel(names, *refs):
+    r = types.SimpleNamespace(**dict(zip(names, refs)))
+    b = lax.axis_index("dp")
+    s = lax.axis_index("seq")
+    z = lax.div(b, 2)
+    y = lax.rem(b, 2)
+    z1 = lax.div(b, 4)
+    z0 = lax.rem(z, 2)
+    x = lax.div(s, 2)
+    c = lax.rem(s, 2)
+    zf = z + 1 - 2 * z0
+    zg = z + 2 - 4 * z1
+    zh = zf + 2 - 4 * z1
+    core = (b, s + 1 - 2 * c)
+    xp = (b, s + 2 - 4 * x)
+    diag = (b, 3 - s)
+    yp = (b + 1 - 2 * y, s)
+    z0p = (b + 2 - 4 * z0, s)
+    z1p = (b + 4 - 8 * z1, s)
+    p1 = (b + c * (2 - 4 * z0), s + (1 - c) * (2 - 4 * x))
+    p2 = (b + (1 - c) * (2 - 4 * z0), s + c * (2 - 4 * x))
+    jme = z0 * 2 + x
+    jx = z0 * 2 + 1 - x
+    jz = (1 - z0) * 2 + x
+    jd = (1 - z0) * 2 + 1 - x
+    jp1 = jx + c * (jz - jx)
+    jp2 = jz + c * (jx - jz)
+    oc = 1 - c
+    oy = 1 - y
+
+    def send(src, dst, ss, rs, dev):
+        pltpu.make_async_remote_copy(
+            src_ref=src, dst_ref=dst, send_sem=ss, recv_sem=rs, device_id=dev, device_id_type=MESH
+        ).start()
+
+    def sent(src, ss):
+        pltpu.make_async_remote_copy(
+            src_ref=src, dst_ref=src, send_sem=ss, recv_sem=ss, device_id=core, device_id_type=MESH
+        ).wait_send()
+
+    def got(dst, rs):
+        pltpu.make_async_remote_copy(
+            src_ref=dst, dst_ref=dst, send_sem=rs, recv_sem=rs, device_id=core, device_id_type=MESH
+        ).wait_recv()
+
+    def ag_first(src, slot, ss, rs):
+        send(src, slot(z, y), ss(0), rs(b), z0p)
+
+    def ag_own(slot, ss, rs):
+        send(slot(z, y), slot(z, y), ss(1), rs(b), z1p)
+        send(slot(z, y), slot(z, y), ss(2), rs(b), yp)
+
+    def ag_z0(slot, ss, rs):
+        k = 2 * zf + y
+        got(slot(zf, y), rs(k))
+        send(slot(zf, y), slot(zf, y), ss(3), rs(k), z1p)
+        send(slot(zf, y), slot(zf, y), ss(4), rs(k), yp)
+
+    def ag_z1(slot, ss, rs):
+        for zz, n in ((zg, 5), (zh, 6)):
+            k = 2 * zz + y
+            got(slot(zz, y), rs(k))
+            send(slot(zz, y), slot(zz, y), ss(n), rs(k), yp)
+
+    def ag_fin(slot, rs):
+        for zz in range(4):
+            got(slot(zz, oy), rs(2 * zz + oy))
+
+    def ag_sent(src, slot, ss):
+        sent(src, ss(0))
+        for n in range(1, 7):
+            sent(slot(z, y), ss(n))
+
+    def tok_own(buf, n):
+        own = buf.at[jme, c]
+        send(own, own, r.tok_s.at[n, 1], r.tok_r.at[n, 1], p1)
+        send(own, own, r.tok_s.at[n, 2], r.tok_r.at[n, 2], p2)
+        send(own, own, r.tok_s.at[n, 0], r.tok_r.at[n, 0], core)
+
+    def tok_relay(buf, n):
+        v = buf.at[jp1, c]
+        got(v, r.tok_r.at[n, 1])
+        send(v, v, r.tok_s.at[n, 3], r.tok_r.at[n, 3], p2)
+        send(v, v, r.tok_s.at[n, 4], r.tok_r.at[n, 4], core)
+        v = buf.at[jp2, c]
+        got(v, r.tok_r.at[n, 2])
+        send(v, v, r.tok_s.at[n, 5], r.tok_r.at[n, 5], core)
+        v = buf.at[jd, c]
+        got(v, r.tok_r.at[n, 3])
+        send(v, v, r.tok_s.at[n, 6], r.tok_r.at[n, 6], core)
+
+    def tok_fin(buf, n):
+        got(buf.at[jme, oc], r.tok_r.at[n, 0])
+        got(buf.at[jp2, oc], r.tok_r.at[n, 4])
+        got(buf.at[jp1, oc], r.tok_r.at[n, 5])
+        got(buf.at[jd, oc], r.tok_r.at[n, 6])
+        for k in range(7):
+            sent(buf.at[jme, c], r.tok_s.at[n, k])
+
+    def sum_first(buf, rc, n):
+        send(buf.at[:, oc], rc, r.sum_s.at[n, 0], r.sum_r.at[n, 0], core)
+
+    def sum_core(buf, rc, rp, n):
+        got(rc, r.sum_r.at[n, 0])
+        for j in range(4):
+            buf[j, c] = (buf[j, c].astype(F32) + rc[j].astype(F32)).astype(BF)
+        send(buf.at[jd, c], rp.at[0], r.sum_s.at[n, 1], r.sum_r.at[n, 1], p2)
+        send(buf.at[jp2, c], rp.at[1], r.sum_s.at[n, 2], r.sum_r.at[n, 2], p2)
+
+    def sum_relay(buf, rp, n):
+        got(rp.at[0], r.sum_r.at[n, 1])
+        buf[jp1, c] = (buf[jp1, c].astype(F32) + rp[0].astype(F32)).astype(BF)
+        send(buf.at[jp1, c], rp.at[2], r.sum_s.at[n, 3], r.sum_r.at[n, 3], p1)
+
+    def sum_fin(buf, rc, rp, n):
+        got(rp.at[1], r.sum_r.at[n, 2])
+        got(rp.at[2], r.sum_r.at[n, 3])
+        total = buf[jme, c].astype(F32) + rp[1].astype(F32) + rp[2].astype(F32)
+        sent(rc, r.sum_s.at[n, 0])
+        for k in range(1, 4):
+            sent(rp.at[0], r.sum_s.at[n, k])
+        return total
+
+    barrier = pltpu.get_barrier_semaphore()
+    peers = (core, xp, diag, yp, z0p, z1p)
+    for dev in peers:
+        pl.semaphore_signal(barrier, inc=1, device_id=dev, device_id_type=MESH)
+
+    def stage_copies():
+        out = []
+        for m in range(4):
+            for zz in range(2):
+                for h in range(2):
+                    for k in range(2):
+                        zt = z0 + zz * (1 - 2 * z0)
+                        col = pl.multiple_of(
+                            h * 2048 + 1024 * k + 512 * zt + 256 * c + 128 * x, 128
+                        )
+                        if m < 3:
+                            src = r.e_in.at[m, :, pl.ds(col, 128)]
+                        else:
+                            src = r.s_in.at[:, pl.ds(col, 128)]
+                        at = (h * 2 + k) * 128
+                        q = 2 * m + zz
+                        dst = r.acc.at[q // 2, q % 2, pl.ds(0, 96), pl.ds(at, 128)]
+                        out.append((src, dst, r.stage_sem.at[m, zz * 4 + h * 2 + k]))
+            row = pl.multiple_of(128 * x, 128)
+            if m < 3:
+                src = r.e_out.at[m, pl.ds(row, 128), :]
+            else:
+                src = r.s_out.at[pl.ds(row, 128), :]
+            dst = r.acc.at[m // 2, m % 2, pl.ds(96, 128), pl.ds(0, D)]
+            out.append((src, dst, r.stage_sem.at[m, 8]))
+        return [pltpu.make_async_copy(*one) for one in out]
+
+    staged = stage_copies()
+    for one in staged:
+        one.start()
+
+    q_slot = lambda zz, yy: r.wq.at[zz, yy]
+    q_ss = lambda n: r.att_s.at[0, n]
+    q_rs = lambda n: r.att_r.at[0, n]
+    o_slot = lambda zz, yy: r.ow.at[zz, yy, c]
+    o_ss = lambda n: r.att_s.at[1, n]
+    o_rs = lambda n: r.att_r.at[1, n]
+    m_slot = lambda zz, yy: r.misc.at[zz, yy]
+    m_ss = lambda n: r.att_s.at[2, n]
+    m_rs = lambda n: r.att_r.at[2, n]
+
+    def w_slot(m):
+        return lambda zz, yy: r.win.at[m, zz, yy]
+
+    def w_ss(m):
+        return lambda n: r.w_s.at[m, n]
+
+    def w_rs(m):
+        return lambda n: r.w_r.at[m, n]
+
+    r.wq[z, y] = r.wq_in[...]
+    r.misc[z, y] = r.misc_in[...]
+    r.ow[z, y, c] = r.ow_in[...]
+    r.nall[s] = r.x_in[...]
+    r.cota[jme, c] = r.cot_in[...]
+
+    pl.semaphore_wait(barrier, len(peers))
+
+    send(r.x_in, r.nall.at[s], r.x_s.at[0], r.x_r.at[0], core)
+    send(r.x_in, r.nall.at[s], r.x_s.at[1], r.x_r.at[1], xp)
+    att_sets = (
+        (r.misc_in, m_slot, m_ss, m_rs),
+        (r.wq_in, q_slot, q_ss, q_rs),
+        (r.ow_in, o_slot, o_ss, o_rs),
+    )
+    for src, slot, ss, rs in att_sets:
+        ag_first(src, slot, ss, rs)
+        ag_own(slot, ss, rs)
+
+    for one in staged:
+        one.wait()
+    for m in range(4):
+        q = 2 * m
+        r.win[m, z, y] = r.acc[q // 2, q % 2, 0:96, 0:512].astype(BF)
+        q = 2 * m + 1
+        r.dg[m, 0:96, :] = r.acc[q // 2, q % 2, 0:96, 0:512].astype(BF)
+        ag_first(r.dg.at[m, pl.ds(0, 96)], w_slot(m), w_ss(m), w_rs(m))
+
+    @pl.when(c == y)
+    def _():
+        for m in range(4):
+            r.wout[m, z1] = r.acc[m // 2, m % 2, 96:224, 0:D].astype(BF)
+
+    xf = s + 2 - 4 * x
+    got(r.nall.at[xf], r.x_r.at[1])
+    send(r.nall.at[xf], r.nall.at[xf], r.x_s.at[2], r.x_r.at[2], core)
+    for src, slot, ss, rs in att_sets:
+        ag_z0(slot, ss, rs)
+    for src, slot, ss, rs in att_sets:
+        ag_z1(slot, ss, rs)
+    tok_own(r.cota, 0)
+    for src, slot, ss, rs in att_sets[:2]:
+        ag_fin(slot, rs)
+
+    def w_own(m):
+        ag_own(w_slot(m), w_ss(m), w_rs(m))
+
+        @pl.when(c == y)
+        def _():
+            v = r.wout.at[m, z1]
+            send(v, v, r.o_s.at[m, 0], r.o_r.at[m, z1], z1p)
+            send(v, v, r.o_s.at[m, 1], r.o_r.at[m, z1], yp)
+
+    def w_relay(m):
+        ag_z0(w_slot(m), w_ss(m), w_rs(m))
+
+    def w_relay_far(m):
+        ag_z1(w_slot(m), w_ss(m), w_rs(m))
+
+        @pl.when(c == y)
+        def _():
+            v = r.wout.at[m, 1 - z1]
+            got(v, r.o_r.at[m, 1 - z1])
+            send(v, v, r.o_s.at[m, 2], r.o_r.at[m, 1 - z1], yp)
+
+    def w_fin(m):
+        ag_fin(w_slot(m), w_rs(m))
+
+        @pl.when(c != y)
+        def _():
+            got(r.wout.at[m, 0], r.o_r.at[m, 0])
+            got(r.wout.at[m, 1], r.o_r.at[m, 1])
+
+        for n in range(1, 7):
+            sent(r.win.at[m, z, y], r.w_s.at[m, n])
+
+        @pl.when(c == y)
+        def _():
+            for k in range(3):
+                sent(r.wout.at[m, 0], r.o_s.at[m, k])
+
+    for m in range(4):
+        w_own(m)
+
+    rows = jnp.zeros((8, D), F32)
+    for k in range(8):
+        row_i = lax.broadcasted_iota(jnp.int32, (128, D), 0)
+        col_i = lax.broadcasted_iota(jnp.int32, (128, D), 1)
+        place = jnp.where((col_i == row_i + 96 * k) & (row_i < 96), 1.0, 0.0).astype(BF)
+        rows = rows + nn(r.misc[k // 2, k % 2].astype(BF), place)
+    r.mrow[...] = rows
+    row8 = lax.broadcasted_iota(jnp.int32, (8, D), 0)
+    r.rpad[...] = jnp.zeros((128, D), BF)
+    r.rpad[0:16, :] = jnp.concatenate(
+        [jnp.where(row8 < 3, rows, 0.0), jnp.zeros((8, D), F32)], axis=0
+    ).astype(BF)
+
+    got(r.nall.at[s + 1 - 2 * c], r.x_r.at[0])
+    got(r.nall.at[3 - s], r.x_r.at[2])
+    for k in range(3):
+        sent(r.x_in, r.x_s.at[k])
+    wq = r.wq[...].reshape(D, QKV_PAD)
+    lane128 = lax.broadcasted_iota(jnp.int32, (TOK, 128), 1)
+
+    def project(t, carry):
+        xv = r.nall[t].astype(F32)
+        r1 = lax.rsqrt(jnp.mean(xv * xv, axis=-1, keepdims=True) + EPSILON)
+        nb = (xv * r1 * r.mrow[3:4, :]).astype(BF)
+        r.nall[t] = nb
+        pr = nn(nb, r.wq[...].reshape(D, QKV_PAD))
+        at = pl.ds(pl.multiple_of(t * TOK, TOK), TOK)
+        cosv = r.cos_in[at, :]
+        sinv = r.sin_in[at, :]
+        for h in range(3):
+            g = pr[:, 128 * h : 128 * h + 128]
+            g = (g * cosv + swap_halves(g) * sinv).astype(BF).astype(F32)
+            g = jnp.where(lane128 < 64, g * 0.125, g)
+            r.kq[h, at, :] = pltpu.roll(g, 64, 1).astype(BF)
+        r.val[0, at, :] = pr[:, 384:512].astype(BF)
+        r.val[1, at, :] = pr[:, 512:640].astype(BF)
+        return carry
+
+    lax.fori_loop(0, 4, project, 0)
+
+    for m in range(4):
+        w_relay(m)
+    tok_relay(r.cota, 0)
+
+    for i in range(3, -1, -1):
+        n = (i + 1) * TOK
+        base = i * (i + 1) // 2
+
+        def heads(h, carry, i=i, n=n, base=base):
+            q = pltpu.roll(r.kq[h, i * TOK : i * TOK + TOK, :].astype(F32), 64, 1)
+            q = jnp.where(lane128 < 64, q, 0.0)
+            sc = nt(q.astype(BF), r.kq[h, 0:n, :])
+            top = jnp.max(sc, axis=-1, keepdims=True)
+            e = jnp.exp(sc - top)
+            pb = (e * (1.0 / jnp.sum(e, axis=-1, keepdims=True))).astype(BF)
+            for j in range(i + 1):
+                r.prob[h, base + j] = pb[:, j * TOK : j * TOK + TOK]
+            r.acc[h, 0, :, 0:128] = nn(pb, r.val[lax.div(h, 2), 0:n, :])
+            return carry
+
+        lax.fori_loop(0, 3, heads, 0)
+        r.att[i, :, 0:128] = jnp.where(lane128 < 64, r.acc[0, 0, :, 0:128], r.acc[1, 0, :, 0:128]).astype(BF)
+        r.att[i, :, 128:256] = r.acc[2, 0, :, 0:128].astype(BF)
+
+        @pl.when(s != i)
+        def _(i=i):
+            send(r.att.at[i], r.arow.at[s], r.a_s.at[i], r.a_r.at[s], (b, i))
+
+        @pl.when(s == i)
+        def _(i=i):
+            r.arow[i] = r.att[i]
+
+        if i == 3:
+            ag_fin(o_slot, o_rs)
+            send(r.ow.at[:, :, c], r.ow.at[:, :, c], r.ow_s.at[0], r.ow_r.at[0], core)
+        if i == 2:
+            w_relay_far(0)
+        if i == 0:
+            w_relay_far(1)
+
+    got(r.ow.at[:, :, oc], r.ow_r.at[0])
+    sent(r.ow.at[:, :, c], r.ow_s.at[0])
+    for src, slot, ss, rs in att_sets:
+        ag_sent(src, slot, ss)
+    for i in range(4):
+
+        @pl.when(s != i)
+        def _(i=i):
+            got(r.arow.at[i], r.a_r.at[i])
+            sent(r.att.at[i], r.a_s.at[i])
+
+    ow = r.ow[...].reshape(D, D)
+    mid = r.x_in[...].astype(F32)
+    for i in range(4):
+        mid = mid + nn(r.arow[i][:, 0:192], ow[192 * i : 192 * i + 192, :])
+    r.mid[...] = mid
+    r2 = lax.rsqrt(jnp.mean(mid * mid, axis=-1, keepdims=True) + EPSILON)
+    nb = (mid * r2 * r.mrow[4:5, :]).astype(BF)
+    r.nown[...] = nb
+    r.nta[jme, c, :, 0:D] = nb
+    r.nta[jme, c, :, D : D + 128] = r.sel_in[...]
+    tok_own(r.nta, 1)
+    tok_fin(r.cota, 0)
+    tok_relay(r.nta, 1)
+    tok_fin(r.nta, 1)
+
+    def gates(sel, nv):
+        lg = nt(nv, r.rpad[...])
+        lg = jnp.where(lane128 < 3, lg, -1e30)
+        e = jnp.exp(lg - jnp.max(lg, axis=-1, keepdims=True))
+        return e / jnp.sum(e, axis=-1, keepdims=True)
+
+    def route(g, carry):
+        j = lax.div(g, 2)
+        k = lax.rem(g, 2)
+        sel = r.nta[j, k, :, D : D + 128].astype(F32)
+        pv = gates(sel, r.nta[j, k, :, 0:D])
+        r.gate[g] = jnp.where(lane128 < 3, pv * sel, sel)
+        r.acc[j, k] = jnp.zeros((TOK, D + 128), F32)
+        return carry
+
+    lax.fori_loop(0, 8, route, 0)
+    r.pown[...] = gates(None, r.nown[...])
+
+    def rs_first(m):
+        send(r.win.at[m, :, oy], r.ry_in.at[m], r.rs_s.at[m, 0], r.rs_r.at[m, 0], yp)
+
+        @pl.when(c != y)
+        def _():
+            send(r.gout.at[m], r.ry_out.at[m], r.rs_s.at[m, 1], r.rs_r.at[m, 1], yp)
+
+    def rs_y(m):
+        got(r.ry_in.at[m], r.rs_r.at[m, 0])
+        for zz in range(4):
+            r.win[m, zz, y] = (r.win[m, zz, y].astype(F32) + r.ry_in[m, zz].astype(F32)).astype(BF)
+        send(
+            r.win.at[m, pl.ds(2 - 2 * z1, 2), y], r.rz_in.at[m], r.rs_s.at[m, 2], r.rs_r.at[m, 2], z1p
+        )
+
+        @pl.when(c == y)
+        def _():
+            got(r.ry_out.at[m], r.rs_r.at[m, 1])
+            for k in range(2):
+                r.gout[m, k] = (r.gout[m, k].astype(F32) + r.ry_out[m, k].astype(F32)).astype(BF)
+            send(r.gout.at[m, 1 - z1], r.rz_out.at[m], r.rs_s.at[m, 3], r.rs_r.at[m, 3], z1p)
+
+    def rs_z(m):
+        got(r.rz_in.at[m], r.rs_r.at[m, 2])
+        for k in range(2):
+            zz = 2 * z1 + k
+            r.win[m, zz, y] = (r.win[m, zz, y].astype(F32) + r.rz_in[m, k].astype(F32)).astype(BF)
+        send(r.win.at[m, zf, y], r.g_in.at[m, s, z0], r.rs_s.at[m, 4], r.rs_r.at[m, 4], z0p)
+        pltpu.make_async_copy(r.win.at[m, z, y], r.g_in.at[m, s, z0], r.loc.at[m, 0]).start()
+
+        @pl.when(c == y)
+        def _():
+            got(r.rz_out.at[m], r.rs_r.at[m, 3])
+            v = (r.gout[m, z1].astype(F32) + r.rz_out[m].astype(F32)).astype(BF)
+            r.gout[m, z1] = v
+            g = r.gout.at[m, z1]
+            pltpu.make_async_copy(g, r.g_out.at[m, x], r.loc.at[m, 1]).start()
+            send(g, r.g_out.at[m, x], r.rs_s.at[m, 5], r.rs_r.at[m, 5], xp)
+            send(g, r.g_out.at[m, x], r.rs_s.at[m, 6], r.rs_r.at[m, 6], core)
+
+    def rs_join(m):
+        got(r.g_in.at[m, s, 1 - z0], r.rs_r.at[m, 4])
+        pltpu.make_async_copy(r.win.at[m, z, y], r.g_in.at[m, s, z0], r.loc.at[m, 0]).wait()
+        g = r.g_in.at[m, s]
+        send(g, g, r.rs_s.at[m, 7], r.rs_r.at[m, 7], xp)
+        send(g, g, r.rs_s.at[m, 8], r.rs_r.at[m, 8], core)
+
+    def rs_spread(m):
+        g = r.g_in.at[m, xf]
+        got(g, r.rs_r.at[m, 7])
+        send(g, g, r.rs_s.at[m, 9], r.rs_r.at[m, 9], core)
+
+        @pl.when(c == y)
+        def _():
+            v = r.g_out.at[m, 1 - x]
+            got(v, r.rs_r.at[m, 5])
+            send(v, v, r.rs_s.at[m, 10], r.rs_r.at[m, 10], core)
+
+    def rs_end(m):
+        got(r.g_in.at[m, s + 1 - 2 * c], r.rs_r.at[m, 8])
+        got(r.g_in.at[m, 3 - s], r.rs_r.at[m, 9])
+        sent(r.ry_in.at[m], r.rs_s.at[m, 0])
+        sent(r.rz_in.at[m], r.rs_s.at[m, 2])
+        sent(r.win.at[m, zf, y], r.rs_s.at[m, 4])
+        for k in (7, 8, 9):
+            sent(r.g_in.at[m, s], r.rs_s.at[m, k])
+
+        @pl.when(c != y)
+        def _():
+            sent(r.gout.at[m], r.rs_s.at[m, 1])
+            got(r.g_out.at[m, x], r.rs_r.at[m, 6])
+            got(r.g_out.at[m, 1 - x], r.rs_r.at[m, 10])
+
+        @pl.when(c == y)
+        def _():
+            g = r.gout.at[m, z1]
+            pltpu.make_async_copy(g, r.g_out.at[m, x], r.loc.at[m, 1]).wait()
+            for k in (3, 5, 6, 10):
+                sent(g, r.rs_s.at[m, k])
+
+    def feed(m, carry):
+        @pl.when(m < 2)
+        def _():
+            w_relay_far(m + 2)
+
+        w_fin(m)
+
+        def tokens(g, inner):
+            j = lax.div(g, 2)
+            k = lax.rem(g, 2)
+            w = r.win[m].reshape(D, 512)
+            wo = r.wout[m].reshape(256, D)
+            gu = nn(r.nta[j, k, :, 0:D], w)
+            zv = gu[:, 0:256]
+            uv = gu[:, 256:512]
+            sg = 1.0 / (1.0 + jnp.exp(-zv))
+            sw = zv * sg
+            act = (sw * uv).astype(BF).astype(F32)
+            dr = nt(r.cota[j, k], wo)
+            gv = jnp.sum(jnp.where(lane128 == m, r.gate[g], 0.0), axis=-1, keepdims=True)
+            gg = jnp.sum(act * dr, axis=-1, keepdims=True)
+            r.ga[g, :, pl.ds(pl.multiple_of(m * 256, 256), 256)] = (act * gv).astype(BF)
+            d = dr * gv
+            dg = jnp.concatenate([d * uv * (sg * (1.0 + zv * (1.0 - sg))), d * sw], axis=1).astype(BF)
+            r.dg[g] = dg
+            r.acc[j, k, :, 0:D] += nt(dg, w)
+            r.acc[j, k, :, D : D + 128] += jnp.where(lane128 == m, gg, 0.0)
+            return inner
+
+        lax.fori_loop(0, 8, tokens, 0)
+        nta = r.nta[:, :, :, 0:D].reshape(2048, D)
+        r.win[m] = tn(nta, r.dg[...].reshape(2048, 512)).astype(BF).reshape(4, 2, 96, 512)
+        gam = r.ga[:, :, pl.ds(pl.multiple_of(m * 256, 256), 256)].reshape(2048, 256)
+        r.gout[m] = tn(gam, r.cota[...].reshape(2048, D)).astype(BF).reshape(2, 128, D)
+        rs_first(m)
+
+        @pl.when(m >= 1)
+        def _():
+            rs_y(m - 1)
+
+        @pl.when(m >= 2)
+        def _():
+            rs_z(m - 2)
+
+        return carry
+
+    for m in range(4):
+        sent(r.dg.at[m, pl.ds(0, 96)], r.w_s.at[m, 0])
+    lax.fori_loop(0, 4, feed, 0)
+
+    def pack(g, carry):
+        j = lax.div(g, 2)
+        k = lax.rem(g, 2)
+        r.nta[j, k, :, 0:D] = r.acc[j, k, :, 0:D].astype(BF)
+        v = r.acc[j, k, :, D : D + 128]
+        hi = v.astype(BF).astype(F32)
+        r.nta[j, k, :, D : D + 128] = (hi + pltpu.roll(v - hi, 64, 1)).astype(BF)
+        return carry
+
+    lax.fori_loop(0, 8, pack, 0)
+    sum_first(r.nta, r.ng_c, 0)
+    sum_core(r.nta, r.ng_c, r.ng_p, 0)
+
+    def mix(g, carry):
+        j = lax.div(g, 2)
+        k = lax.rem(g, 2)
+        r.cota[j, k] = nn(r.ga[g], r.wout[...].reshape(1024, D)).astype(BF)
+        return carry
+
+    lax.fori_loop(0, 4, mix, 0)
+    sum_relay(r.nta, r.ng_p, 0)
+    lax.fori_loop(4, 8, mix, 0)
+    rs_y(3)
+    ngs = sum_fin(r.nta, r.ng_c, r.ng_p, 0)
+    sum_first(r.cota, r.out_c, 1)
+
+    upstream = r.cot_in[...].astype(F32)
+    mid = r.mid[...]
+    r2 = lax.rsqrt(jnp.mean(mid * mid, axis=-1, keepdims=True) + EPSILON)
+    gg = ngs[:, D : D + 128]
+    gg = gg + pltpu.roll(gg, 64, 1)
+    pv = r.pown[...]
+    pg = jnp.where(lane128 < 3, gg * r.sel_in[...].astype(F32), 0.0)
+    lg = (pv * (pg - jnp.sum(pv * pg, axis=-1, keepdims=True))).astype(BF)
+    rgrad = tn(lg, r.nown[...])
+    ng = ngs[:, 0:D] + nn(lg, r.rpad[...])
+    gain2 = r.mrow[4:5, :]
+    fgain = jnp.sum(ng * mid * r2, axis=0, keepdims=True)
+    sc = ng * gain2
+    mg = upstream + r2 * sc - mid * (r2 * r2 * r2) * jnp.mean(sc * mid, axis=-1, keepdims=True)
+    r.igrad[...] = mg
+    r.small[...] = jnp.where(row8 < 3, rgrad[0:8, :], 0.0) + jnp.where(row8 == 4, fgain, 0.0)
+    ml = mg.astype(BF)
+    ow = r.ow[...].reshape(D, D)
+    r.att[:, :, 128:256] = jnp.zeros((4, TOK, 128), BF)
+    for i in range(4):
+        da = nt(ml, ow[192 * i : 192 * i + 192, :]).astype(BF)
+        r.att[i, :, 0:192] = da
+
+        @pl.when(s != i)
+        def _(i=i):
+            send(r.att.at[i], r.dat.at[s], r.d_s.at[i], r.d_r.at[s], (b, i))
+
+        @pl.when(s == i)
+        def _(i=i):
+            r.dat[i] = r.att[i]
+
+    for i in range(4):
+        og = tn(r.arow[i][:, 0:192], ml).astype(BF)
+        og = og.reshape(2, 2, 48, D)
+        for k in range(2):
+            r.og[k, i] = og[:, :, :, 384 * k : 384 * k + 384]
+    send(r.og.at[oc], r.og_c, r.og_s.at[0], r.og_r.at[0], core)
+    sum_core(r.cota, r.out_c, r.out_p, 1)
+    for i in range(4):
+
+        @pl.when(s != i)
+        def _(i=i):
+            got(r.dat.at[i], r.d_r.at[i])
+            sent(r.att.at[i], r.d_s.at[i])
+
+    rs_z(2)
+
+    for i in range(4):
+        r.acc[i, 0, :, 0:QKV_PAD] = jnp.zeros((TOK, QKV_PAD), F32)
+    for i in range(3, -1, -1):
+        base = i * (i + 1) // 2
+
+        def heads_back(h, carry, i=i, base=base):
+            hv = lax.div(h, 2)
+            here = lax.div(lane128, 64) == lax.rem(h, 2)
+            vat = pl.ds(pl.multiple_of(hv * 128, 128), 128)
+            cat = pl.ds(pl.multiple_of(384 + hv * 128, 128), 128)
+            hat = pl.ds(pl.multiple_of(h * 128, 128), 128)
+            da = jnp.where(here, r.dat[i, :, vat].astype(F32), 0.0).astype(BF)
+            kqi = r.kq[h, i * TOK : i * TOK + TOK, :].astype(F32)
+            qi = jnp.where(lane128 >= 64, kqi, 0.0).astype(BF)
+            pf = [r.prob[h, base + j] for j in range(i + 1)]
+            dp = [nt(da, r.val[hv, j * TOK : j * TOK + TOK, :]) for j in range(i + 1)]
+            cen = jnp.zeros((TOK, 1), F32)
+            for j in range(i + 1):
+                cen = cen + jnp.sum(pf[j].astype(F32) * dp[j], axis=-1, keepdims=True)
+            dq = jnp.zeros((TOK, 128), F32)
+            for j in range(i + 1):
+                ds = (pf[j].astype(F32) * (dp[j] - cen)).astype(BF)
+                dq = dq + nn(ds, r.kq[h, j * TOK : j * TOK + TOK, :])
+                r.acc[j, 0, :, hat] += tn(ds, qi)
+                r.acc[j, 0, :, cat] += tn(pf[j], da)
+            r.acc[i, 0, :, hat] += jnp.where(lane128 < 64, dq * 0.125, 0.0)
+            return carry
+
+        lax.fori_loop(0, 3, heads_back, 0)
+        cosv = r.cos_in[i * TOK : i * TOK + TOK, :]
+        sinv = r.sin_in[i * TOK : i * TOK + TOK, :]
+        for h in range(3):
+            g = r.acc[i, 0, :, 128 * h : 128 * h + 128].astype(BF).astype(F32)
+            r.nta[i, 0, :, 128 * h : 128 * h + 128] = (g * cosv - swap_halves(g) * sinv).astype(BF)
+        r.nta[i, 0, :, 384:640] = r.acc[i, 0, :, 384:640].astype(BF)
+        r.ng1[i // 2, i % 2] = nt(r.nta[i, 0, :, 0:QKV_PAD], r.wq[...].reshape(D, QKV_PAD)).astype(BF)
+        if i == 3:
+            rs_z(3)
+            got(r.og_c, r.og_r.at[0])
+            for k in range(4):
+                r.og[c, k] = (r.og[c, k].astype(F32) + r.og_c[k].astype(F32)).astype(BF)
+            send(r.og.at[c, :, :, 1 - x], r.og_x, r.og_s.at[1], r.og_r.at[1], xp)
+            sum_relay(r.cota, r.out_p, 1)
+        if i == 2:
+            rs_join(0)
+            rs_join(1)
+            got(r.og_x, r.og_r.at[1])
+            for k in range(4):
+                r.og[c, k, :, x] = (r.og[c, k, :, x].astype(F32) + r.og_x[k].astype(F32)).astype(BF)
+            send(r.og.at[c, :, oy, x], r.og_y, r.og_s.at[2], r.og_r.at[2], yp)
+            tot = sum_fin(r.cota, r.out_c, r.out_p, 1)
+            r.out[...] = (r.mid[...] + tot).astype(BF)
+        if i == 1:
+            rs_join(2)
+            rs_spread(0)
+            got(r.og_y, r.og_r.at[2])
+            for k in range(4):
+                r.og[c, k, y, x] = (r.og[c, k, y, x].astype(F32) + r.og_y[k].astype(F32)).astype(BF)
+            send(r.og.at[c, pl.ds(2 - 2 * z1, 2), y, x], r.og_z, r.og_s.at[3], r.og_r.at[3], z1p)
+
+    ng1_c = r.ng_c.at[pl.ds(0, 2), :, pl.ds(0, D)]
+    ng1_x = r.ng_p.at[0, :, pl.ds(0, D)]
+    send(r.ng1.at[:, oc], ng1_c, r.n_s.at[0], r.n_r.at[0], core)
+    wg = tn(r.nall[...].reshape(1024, D), r.nta[:, 0, :, 0:QKV_PAD].reshape(1024, QKV_PAD))
+    r.wq[...] = wg.astype(BF).reshape(4, 2, 96, QKV_PAD)
+    send(r.wq.at[:, oy], r.q_y, r.q_s.at[0], r.q_r.at[0], yp)
+    got(ng1_c, r.n_r.at[0])
+    for k in range(2):
+        r.ng1[k, c] = (r.ng1[k, c].astype(F32) + r.ng_c[k, :, 0:D].astype(F32)).astype(BF)
+    send(r.ng1.at[1 - x, c], ng1_x, r.n_s.at[1], r.n_r.at[1], xp)
+    rs_join(3)
+    for k in range(1, 3):
+        rs_spread(k)
+    got(r.og_z, r.og_r.at[3])
+    for k in range(2):
+        v = r.og[c, 2 * z1 + k, y, x].astype(F32) + r.og_z[k].astype(F32)
+        r.og[c, 2 * z1 + k, y, x] = v.astype(BF)
+    send(r.og.at[c, zf, y, x], r.og_w, r.og_s.at[4], r.og_r.at[4], z0p)
+
+    got(ng1_x, r.n_r.at[1])
+    sent(r.ng1.at[:, oc], r.n_s.at[0])
+    sent(r.ng1.at[1 - x, c], r.n_s.at[1])
+    ng = r.ng1[x, c].astype(F32) + r.ng_p[0, :, 0:D].astype(F32)
+    xv = r.x_in[...].astype(F32)
+    r1 = lax.rsqrt(jnp.mean(xv * xv, axis=-1, keepdims=True) + EPSILON)
+    gain1 = r.mrow[3:4, :]
+    again = jnp.sum(ng * xv * r1, axis=0, keepdims=True)
+    sc = ng * gain1
+    r.igrad[...] = (
+        r.igrad[...] + r1 * sc - xv * (r1 * r1 * r1) * jnp.mean(sc * xv, axis=-1, keepdims=True)
+    )
+    r.small[...] += jnp.where(row8 == 3, again, 0.0)
+
+    def pair_sum(k, dev):
+        r.small_o[k] = r.small[...]
+        send(r.small_o.at[k], r.small_i.at[k], r.sm_s.at[k], r.sm_r.at[k], dev)
+
+    def pair_add(k):
+        got(r.small_i.at[k], r.sm_r.at[k])
+        r.small[...] += r.small_i[k]
+        sent(r.small_o.at[k], r.sm_s.at[k])
+
+    pair_sum(0, core)
+    got(r.q_y, r.q_r.at[0])
+    for k in range(4):
+        r.wq[k, y] = (r.wq[k, y].astype(F32) + r.q_y[k].astype(F32)).astype(BF)
+    send(r.wq.at[pl.ds(2 - 2 * z1, 2), y], r.q_z, r.q_s.at[1], r.q_r.at[1], z1p)
+    pair_add(0)
+    pair_sum(1, xp)
+    got(r.og_w, r.og_r.at[4])
+    r.og[c, z, y, x] = (r.og[c, z, y, x].astype(F32) + r.og_w[...].astype(F32)).astype(BF)
+    ogf = r.og.at[c, z, y, x]
+    r.g_ow[s] = r.og[c, z, y, x]
+    send(ogf, r.g_ow.at[s], r.og_s.at[5], r.og_r.at[5], core)
+    send(ogf, r.g_ow.at[s], r.og_s.at[6], r.og_r.at[6], xp)
+    pair_add(1)
+    pair_sum(2, yp)
+    rs_spread(3)
+    got(r.q_z, r.q_r.at[1])
+    for k in range(2):
+        v = r.wq[2 * z1 + k, y].astype(F32) + r.q_z[k].astype(F32)
+        r.wq[2 * z1 + k, y] = v.astype(BF)
+    send(r.wq.at[zf, y], r.q_w, r.q_s.at[2], r.q_r.at[2], z0p)
+    pair_add(2)
+    pair_sum(3, z1p)
+    got(r.g_ow.at[xf], r.og_r.at[6])
+    send(r.g_ow.at[xf], r.g_ow.at[xf], r.og_s.at[7], r.og_r.at[7], core)
+    got(r.q_w, r.q_r.at[2])
+    r.wq[z, y] = (r.wq[z, y].astype(F32) + r.q_w[...].astype(F32)).astype(BF)
+    r.g_q[s] = r.wq[z, y]
+    send(r.wq.at[z, y], r.g_q.at[s], r.q_s.at[3], r.q_r.at[3], xp)
+    send(r.wq.at[z, y], r.g_q.at[s], r.q_s.at[4], r.q_r.at[4], core)
+    pair_add(3)
+    pair_sum(4, z0p)
+    for m in range(4):
+        rs_end(m)
+    got(r.g_q.at[xf], r.q_r.at[3])
+    send(r.g_q.at[xf], r.g_q.at[xf], r.q_s.at[5], r.q_r.at[5], core)
+    pair_add(4)
+    r.g_small[...] = r.small[...]
+    got(r.g_ow.at[s + 1 - 2 * c], r.og_r.at[5])
+    got(r.g_ow.at[3 - s], r.og_r.at[7])
+    got(r.g_q.at[s + 1 - 2 * c], r.q_r.at[4])
+    got(r.g_q.at[3 - s], r.q_r.at[5])
+    sent(r.og_c, r.og_s.at[0])
+    sent(r.og_x, r.og_s.at[1])
+    sent(r.og_y, r.og_s.at[2])
+    sent(r.og_z, r.og_s.at[3])
+    sent(r.og_w, r.og_s.at[4])
+    for k in (5, 6, 7):
+        sent(r.g_ow.at[0], r.og_s.at[k])
+    sent(r.q_y, r.q_s.at[0])
+    sent(r.q_z, r.q_s.at[1])
+    for k in (2, 3, 4, 5):
+        sent(r.q_w, r.q_s.at[k])
+
+
+def vmem(shape, kind=BF):
+    return pltpu.VMEM(shape, kind)
+
+
+def layer_call(ins, cos_table, sin_table):
+    dma = pltpu.SemaphoreType.DMA
+    in_names = (
+        ["x_in", "cot_in", "wq_in", "misc_in", "ow_in", "sel_in", "cos_in", "sin_in"]
+        + ["e_in", "e_out", "s_in", "s_out"]
+    )
+    out_names = ["out", "igrad", "g_small", "g_q", "g_ow", "g_in", "g_out"]
+    out_shapes = (
+        ((TOK, D), BF),
+        ((TOK, D), F32),
+        ((8, D), F32),
+        ((4, 96, QKV_PAD), BF),
+        ((4, 48, 384), BF),
+        ((4, 4, 2, 96, 512), BF),
+        ((4, 2, 128, D), BF),
+    )
+    scratch = {
+        "nall": vmem((4, TOK, D)),
+        "wq": vmem((4, 2, 96, QKV_PAD)),
+        "misc": vmem((4, 2, 8, 128), F32),
+        "ow": vmem((4, 2, 2, 48, D)),
+        "kq": vmem((3, 1024, 128)),
+        "val": vmem((2, 1024, 128)),
+        "prob": vmem((3, 10, TOK, TOK)),
+        "att": vmem((4, TOK, 256)),
+        "arow": vmem((4, TOK, 256)),
+        "dat": vmem((4, TOK, 256)),
+        "mid": vmem((TOK, D), F32),
+        "nown": vmem((TOK, D)),
+        "pown": vmem((TOK, 128), F32),
+        "mrow": vmem((8, D), F32),
+        "rpad": vmem((128, D)),
+        "nta": vmem((4, 2, TOK, D + 128)),
+        "cota": vmem((4, 2, TOK, D)),
+        "gate": vmem((8, TOK, 128), F32),
+        "win": vmem((4, 4, 2, 96, 512)),
+        "wout": vmem((4, 2, 128, D)),
+        "dg": vmem((8, TOK, 512)),
+        "ga": vmem((8, TOK, 1024)),
+        "acc": vmem((4, 2, TOK, D + 128), F32),
+        "gout": vmem((4, 2, 128, D)),
+        "ry_in": vmem((4, 4, 96, 512)),
+        "ry_out": vmem((4, 2, 128, D)),
+        "rz_in": vmem((4, 2, 96, 512)),
+        "rz_out": vmem((4, 128, D)),
+        "ng_c": vmem((4, TOK, D + 128)),
+        "ng_p": vmem((3, TOK, D + 128)),
+        "out_c": vmem((4, TOK, D)),
+        "out_p": vmem((3, TOK, D)),
+        "ng1": vmem((2, 2, TOK, D)),
+        "og": vmem((2, 4, 2, 2, 48, 384)),
+        "og_c": vmem((4, 2, 2, 48, 384)),
+        "og_x": vmem((4, 2, 48, 384)),
+        "og_y": vmem((4, 48, 384)),
+        "og_z": vmem((2, 48, 384)),
+        "og_w": vmem((48, 384)),
+        "q_y": vmem((4, 96, QKV_PAD)),
+        "q_z": vmem((2, 96, QKV_PAD)),
+        "q_w": vmem((96, QKV_PAD)),
+        "small": vmem((8, D), F32),
+        "small_o": vmem((5, 8, D), F32),
+        "small_i": vmem((5, 8, D), F32),
+        "stage_sem": dma((4, 9)),
+        "att_s": dma((3, 7)),
+        "att_r": dma((3, 8)),
+        "w_s": dma((4, 7)),
+        "w_r": dma((4, 8)),
+        "o_s": dma((4, 3)),
+        "o_r": dma((4, 2)),
+        "ow_s": dma((1,)),
+        "ow_r": dma((1,)),
+        "x_s": dma((3,)),
+        "x_r": dma((3,)),
+        "tok_s": dma((2, 7)),
+        "tok_r": dma((2, 7)),
+        "a_s": dma((4,)),
+        "a_r": dma((4,)),
+        "d_s": dma((4,)),
+        "d_r": dma((4,)),
+        "sum_s": dma((2, 4)),
+        "sum_r": dma((2, 4)),
+        "rs_s": dma((4, 11)),
+        "rs_r": dma((4, 11)),
+        "loc": dma((4, 2)),
+        "og_s": dma((8,)),
+        "og_r": dma((8,)),
+        "q_s": dma((6,)),
+        "q_r": dma((6,)),
+        "n_s": dma((2,)),
+        "n_r": dma((2,)),
+        "sm_s": dma((5,)),
+        "sm_r": dma((5,)),
+    }
+    names = in_names + out_names + list(scratch)
+    in_vmem = pl.BlockSpec(memory_space=pltpu.VMEM)
+    in_any = pl.BlockSpec(memory_space=pl.ANY)
+    return pl.pallas_call(
+        functools.partial(layer_kernel, names),
+        out_shape=[jax.ShapeDtypeStruct(*one) for one in out_shapes],
+        in_specs=[in_vmem] * 8 + [in_any] * 4,
+        out_specs=[in_vmem] * 5 + [in_any] * 2,
+        scratch_shapes=list(scratch.values()),
+        compiler_params=pltpu.CompilerParams(
+            collective_id=0, has_side_effects=True, vmem_limit_bytes=VMEM_LIMIT
+        ),
+        cost_estimate=pl.CostEstimate(
+            flops=35_000_000_000, bytes_accessed=60_000_000, transcendentals=6_000_000
+        ),
+        name="layer",
+    )(*ins[:6], cos_table, sin_table, *ins[6:])
+
+
+def fast_device(
+    inputs,
+    attn_gain,
+    qkv_weight,
+    out_weight,
+    ffn_gain,
+    router_weight,
+    expert_in,
+    expert_out,
+    shared_in,
+    shared_out,
+    routes,
+    slot_index,
+    cotangent,
+):
+    b = lax.axis_index("dp")
+    s = lax.axis_index("seq")
+    c = s % 2
+    mine = lax.dynamic_slice_in_dim(qkv_weight, 3 * s, 3, axis=1).astype(BF)
+    pairs = mine[:, :, 0:2].reshape(96, 384)
+    values = mine[:, :, 2].reshape(96, 192)
+    wq = jnp.concatenate([pairs, values, jnp.zeros((96, 64), BF)], axis=1)
+    misc = jnp.concatenate(
+        [router_weight.T, attn_gain[None], ffn_gain[None], jnp.zeros((3, 96), F32)], axis=0
+    )
+    misc = jnp.pad(misc.astype(BF).astype(F32), ((0, 0), (0, 32)))
+    half = lax.dynamic_slice_in_dim(out_weight, 48 * c, 48, axis=0).astype(BF)
+    lane = jnp.arange(128, dtype=jnp.int32)
+    route = routes[0]
+    sel = (lane == route[:, 0:1]) | (lane == route[:, 1:2]) | (lane == 3)
+    sel = sel.astype(BF)
+    angle = np.arange(1024, dtype=np.float32)[:, None] * (
+        np.float32(10000.0) ** (-np.arange(32, dtype=np.float32) / np.float32(32))
+    )
+    cos_table = jnp.asarray(np.tile(np.cos(angle), (1, 4)).astype(np.float32))
+    sine = np.sin(angle)
+    sin_table = jnp.asarray(np.tile(np.concatenate([-sine, sine], 1), (1, 2)).astype(np.float32))
+    out, igrad, small, g_q, g_ow, g_in, g_out = layer_call(
+        (
+            inputs[0],
+            cotangent[0],
+            wq,
+            misc,
+            half,
+            sel,
+            expert_in,
+            expert_out,
+            shared_in,
+            shared_out,
+        ),
+        cos_table,
+        sin_table,
+    )
+    shard = lax.dynamic_slice_in_dim(small, 96 * b, 96, axis=1)
+    pairs = g_q[:, :, 0:384].reshape(4, 96, 3, 2, 64)
+    values = g_q[:, :, 384:576].reshape(4, 96, 3, 1, 64)
+    qkv_grad = jnp.concatenate([pairs, values], axis=3).transpose(1, 0, 2, 3, 4)
+    qkv_grad = qkv_grad.reshape(96, HEADS, 3, HEAD_DIM).astype(F32)
+    ow_grad = g_ow.reshape(2, 2, 48, 384).transpose(0, 2, 1, 3).reshape(96, D).astype(F32)
+    g = g_in.reshape(4, 2, 2, 2, 96, 2, 2, 128).transpose(0, 4, 5, 6, 3, 2, 1, 7)
+    g = g.reshape(4, 96, 2 * FF).astype(F32)
+    go = g_out.reshape(4, 256, D).astype(F32)
+    return (
+        out[None],
+        igrad[None],
+        shard[3],
+        qkv_grad,
+        ow_grad,
+        shard[4],
+        shard[0:3].T,
+        g[:3],
+        go[:3],
+        g[3],
+        go[3],
+    )
+
+
 def solution(mesh):
+    fits = mesh.shape["dp"] == 8 and mesh.shape["seq"] == 4
     return jax.shard_map(
-        on_device,
+        fast_device if fits else on_device,
         mesh=mesh,
         in_specs=(
             P("dp", "seq", None),

time: 1850 us -> 327 us (0.18)
  waiting for transfers between devices: 1420 us -> 0 us
  Pallas kernels: 0 us -> 280 us
  matrix products: 147 us -> 0 us
  blocking collectives: 97.4 us -> 0 us
  other arithmetic: 56.9 us -> 4.67 us
  local copies, waits for them, and re-layouts: 85.9 us -> 41.3 us
    all_gather x8 -> x0, waiting for transfers between devices: 684 us -> none  [the longest x1 297 us: on_device(): lax.all_gather(ffn_local[2], 'dp', axis=1, tiled=True)]
    reduce_scatter x10 -> x0, waiting for transfers between devices: 520 us -> none  [the longest x1 98.4 us: on_device(): lax.psum_scatter(parts[2], 'dp', scatter_dimension=1, tiled=True)]
    pallas_call x0 -> x1, Pallas kernels: none -> 280 us  [layer_call(): pl.pallas_call(functools.partial(layer_kernel, names), out_shape=[jax.Sha...]
    unnamed x24 -> x0, waiting for transfers between devices: 142 us -> none
    dot_general x32 -> x0, matrix products: 141 us -> none  [the longest x1 13.9 us: on_device(): jnp.einsum('ecd,edf->ecf', buffer, exp_in_full, preferred_element_type=jn...]
    all_to_all x4 -> x0, waiting for transfers between devices: 73.1 us -> none  [the longest x1 46.9 us: on_device(): lax.all_to_all(stacked, 'seq', split_axis=0, concat_axis=1, tiled=True)]
    all_gather x5 -> x0, blocking collectives: 46.5 us -> none  [the longest x1 17.8 us: on_device(): lax.all_gather(ffn_local[1], 'dp', axis=0, tiled=True)]
    unnamed x2 -> x0, blocking collectives: 44.4 us -> none
  transfers between devices with their start and end apart: 25 -> 0, of which waited for: 22 -> 0; matrix products, arithmetic and copies ran while one was open for 15% -> 0% of each run, Pallas kernels for 0% -> 0%
where the time goes in v1:
time: 327 us; the launch traced here: 326 us
  Pallas kernels  280 us (86%)
  local copies, waits for them, and re-layouts  41.3 us (13%)
  other arithmetic  4.67 us (1%)
    pallas_call x1, Pallas kernels, layer_call(): pl.pallas_call(functools.partial(layer_kernel, names), out_shape=[jax.Sha...  280 us
    slice x3, local copies, waits for them, and re-layouts, fast_device(): g[:3]  16.9 us

profile of v1, /device:TPU:0, one launch (start us, length us, event | category | flops | bytes accessed | tf_op | source)
XLA Modules:
  0.0 326.3 jit_solution(5088319204650172510)
XLA Ops:
  0.6 0.0 copy-start
  0.7 0.1 pad.13.clone
  0.8 0.7 convert_bitcast_fusion.1
  1.5 0.7 convert_bitcast_fusion.2
  2.1 0.1 maximum_maximum_fusion.1
  2.2 0.1 pad.16.clone
  2.3 0.6 pad_convert_fusion.refs_3_
  2.9 0.8 fusion.3
  3.6 0.8 fusion.2.refs_5_
  4.4 0.0 copy-done
  4.4 0.6 dynamic-slice_convert_fusion.refs_4_
  5.1 1.0 constant_dynamic-slice_fusion.1
  6.1 0.1 copy.34
  6.2 0.1 copy.35
  6.3 0.7 maximum_maximum_fusion.refs_2_
  7.0 279.5 %layer.1 = (bf16[256,768]{1,0:T(8,128)(2,1)}, f32[256,768]{1,0:T(8,128)}, f32[8,768]{1,0:T(8,128)}, bf16[4,96,640]{2,1,0:T(8,128)(2,1)}, bf16[4,48,384]{2,1,0:T(...) custom-call(bf16[256,768]{1,0:T(8,128)(2,1)} %bitcast.57, bf16[256,768]{1,0:T(8,128)(2,1)} %bitcast.58, ...), custom_call_target="tpu_custom_call" | custom-call | flops 35000000512 | bytes 60000000 | tf_op jit(solution)/shard_map/layer/pallas_call | solution.py:1325
  286.5 0.0 copy-start.5
  286.5 0.8 constant_dynamic-slice_fusion
  287.4 0.5 slice_bitcast_fusion.1
  287.9 0.6 slice_bitcast_fusion
  288.5 0.9 slice.53
  289.4 1.0 slice.52
  290.4 0.2 copy.37
  290.6 0.2 copy.36
  290.8 0.0 copy-done.5
  290.8 0.0 copy-start.1
  290.9 0.2 copy.39
  291.0 0.7 copy.43
  291.7 1.2 maximum_convert_fusion
  292.9 0.0 copy-done.1
  292.9 0.9 slice.69
  293.8 0.0 copy-start.2
  293.9 1.6 slice.67
  295.5 1.1 copy-done.2
  296.6 5.6 %reshape.62 = f32[4,2,2,2,96,2,2,128]{7,6,5,4,3,2,1,0:T(2,128)} reshape(bf16[4,4,2,96,512]{4,3,2,1,0:T(8,128)(2,1)S(1)} %copy-done.2) | data formatting | bytes 9437184 | tf_op jit(solution)/shard_map/convert_element_type | solution.py:1401
  302.2 1.9 slice.68
  304.1 4.0 %slice.66 = f32[3,96,2,2,2,2,2,128]{7,3,2,1,4,5,6,0:T(2,128)S(1)} slice(f32[4,96,2,2,2,2,2,128]{7,3,2,1,4,5,6,0:T(2,128)} %bitcast.41), slice={[0:3], [0:96], [0:2], [0:2], [0:2], [0:2], [0:2], [0:128]} | slice | bytes 9437184 | tf_op jit(solution)/shard_map/slice | solution.py:1411
  308.1 5.8 %copy.40 = f32[3,96,2,2,2,2,2,128]{7,6,5,4,3,2,1,0:T(2,128)} copy(f32[3,96,2,2,2,2,2,128]{7,3,2,1,4,5,6,0:T(2,128)S(1)} %slice.66) | data formatting | bytes 9437184 | tf_op jit(solution)/shard_map/slice | solution.py:1411
  313.9 7.2 %slice.57 = f32[3,96,4096]{2,1,0:T(8,128)} reshape(f32[3,96,2,2,2,2,2,128]{7,6,5,4,3,2,1,0:T(2,128)} %copy.40) | data formatting | bytes 9437184 | tf_op jit(solution)/shard_map/slice | solution.py:1411
  321.1 1.2 copy.41
  322.3 0.0 copy-start.4
  322.3 0.0 copy-start.3
  322.3 2.4 squeeze.26
  324.7 0.0 copy-done.4
  324.7 0.7 copy.50
  325.5 0.0 copy-done.3
  325.5 0.9 copy.51
  (9 shorter events, 0.1 us)
Async XLA Ops:
  0.6 3.8 %copy-start = (f32[96,768]{1,0:T(8,128)S(1)}, f32[96,768]{1,0:T(8,128)}, u32[]{:S(2)}) copy-start(f32[96,768]{1,0:T(8,128)} %param.18) | copy-start | bytes 884740
  286.5 4.3 %copy-start.5 = (bf16[4,48,384]{2,1,0:T(8,128)(2,1)S(1)}, bf16[4,48,384]{2,1,0:T(8,128)(2,1)}, u32[]{:S(2)}) copy-start(bf16[4,48,384]{2,1,0:T(8,128)(2,1)} %get-tuple-element.22) | copy-start | bytes 442372
  290.8 2.1 copy-start.1
  293.8 2.7 copy-start.2
  322.3 2.4 copy-start.4
  322.3 3.2 copy-start.3

commit v2 on v1

--- a/solution.py
+++ b/solution.py
@@ -549,31 +549,46 @@
         for n in range(1, 7):
             sent(slot(z, y), ss(n))
 
-    def tok_own(buf, n):
-        own = buf.at[jme, c]
-        send(own, own, r.tok_s.at[n, 1], r.tok_r.at[n, 1], p1)
-        send(own, own, r.tok_s.at[n, 2], r.tok_r.at[n, 2], p2)
-        send(own, own, r.tok_s.at[n, 0], r.tok_r.at[n, 0], core)
-
-    def tok_relay(buf, n):
-        v = buf.at[jp1, c]
-        got(v, r.tok_r.at[n, 1])
-        send(v, v, r.tok_s.at[n, 3], r.tok_r.at[n, 3], p2)
-        send(v, v, r.tok_s.at[n, 4], r.tok_r.at[n, 4], core)
-        v = buf.at[jp2, c]
+    def tok_own(slot, n):
+        own = slot(jme, c)
+        send(own, own, r.tok_s.at[n, 1], r.tok_r.at[n, 2], p1)
+        send(own, own, r.tok_s.at[n, 2], r.tok_r.at[n, 4], p2)
+        send(own, own, r.tok_s.at[n, 0], r.tok_r.at[n, 1], core)
+
+    def tok_near(slot, n):
+        v = slot(jp1, c)
         got(v, r.tok_r.at[n, 2])
-        send(v, v, r.tok_s.at[n, 5], r.tok_r.at[n, 5], core)
-        v = buf.at[jd, c]
-        got(v, r.tok_r.at[n, 3])
-        send(v, v, r.tok_s.at[n, 6], r.tok_r.at[n, 6], core)
-
-    def tok_fin(buf, n):
-        got(buf.at[jme, oc], r.tok_r.at[n, 0])
-        got(buf.at[jp2, oc], r.tok_r.at[n, 4])
-        got(buf.at[jp1, oc], r.tok_r.at[n, 5])
-        got(buf.at[jd, oc], r.tok_r.at[n, 6])
+        send(v, v, r.tok_s.at[n, 3], r.tok_r.at[n, 6], p2)
+        send(v, v, r.tok_s.at[n, 4], r.tok_r.at[n, 5], core)
+        v = slot(jp2, c)
+        got(v, r.tok_r.at[n, 4])
+        send(v, v, r.tok_s.at[n, 5], r.tok_r.at[n, 3], core)
+
+    def tok_far(slot, n):
+        v = slot(jd, c)
+        got(v, r.tok_r.at[n, 6])
+        send(v, v, r.tok_s.at[n, 6], r.tok_r.at[n, 7], core)
+
+    def tok_fin(slot, n):
+        got(slot(jme, oc), r.tok_r.at[n, 1])
+        got(slot(jp1, oc), r.tok_r.at[n, 3])
+        got(slot(jp2, oc), r.tok_r.at[n, 5])
+        got(slot(jd, oc), r.tok_r.at[n, 7])
+
+    def tok_sent(slot, n):
         for k in range(7):
-            sent(buf.at[jme, c], r.tok_s.at[n, k])
+            sent(slot(jme, c), r.tok_s.at[n, k])
+
+    cot_slot = lambda j, k: r.cota.at[j, k]
+    sel_slot = lambda j, k: r.nta.at[j, k, :, pl.ds(D, 128)]
+    two_slot = lambda j, k: r.nta.at[j, k, :, pl.ds(0, D)]
+
+    def block_at(q):
+        q1 = lax.rem(q, 2)
+        q2 = lax.div(q, 2)
+        fx = q1 + c * (q2 - q1)
+        fz = q2 + c * (q1 - q2)
+        return 2 * (z0 + fz * (1 - 2 * z0)) + x + fx * (1 - 2 * x)
 
     def sum_first(buf, rc, n):
         send(buf.at[:, oc], rc, r.sum_s.at[n, 0], r.sum_r.at[n, 0], core)
@@ -581,7 +596,8 @@
     def sum_core(buf, rc, rp, n):
         got(rc, r.sum_r.at[n, 0])
         for j in range(4):
-            buf[j, c] = (buf[j, c].astype(F32) + rc[j].astype(F32)).astype(BF)
+            v = buf[j, c].astype(F32) + rc[j].astype(F32)
+            buf[j, c] = v.astype(BF)
         send(buf.at[jd, c], rp.at[0], r.sum_s.at[n, 1], r.sum_r.at[n, 1], p2)
         send(buf.at[jp2, c], rp.at[1], r.sum_s.at[n, 2], r.sum_r.at[n, 2], p2)
 
@@ -659,16 +675,14 @@
     r.ow[z, y, c] = r.ow_in[...]
     r.nall[s] = r.x_in[...]
     r.cota[jme, c] = r.cot_in[...]
+    r.nta[jme, c, :, D : D + 128] = r.sel_in[...]
 
     pl.semaphore_wait(barrier, len(peers))
 
     send(r.x_in, r.nall.at[s], r.x_s.at[0], r.x_r.at[0], core)
     send(r.x_in, r.nall.at[s], r.x_s.at[1], r.x_r.at[1], xp)
-    att_sets = (
-        (r.misc_in, m_slot, m_ss, m_rs),
-        (r.wq_in, q_slot, q_ss, q_rs),
-        (r.ow_in, o_slot, o_ss, o_rs),
-    )
+    ow_set = (r.ow_in, o_slot, o_ss, o_rs)
+    att_sets = ((r.misc_in, m_slot, m_ss, m_rs), (r.wq_in, q_slot, q_ss, q_rs))
     for src, slot, ss, rs in att_sets:
         ag_first(src, slot, ss, rs)
         ag_own(slot, ss, rs)
@@ -680,7 +694,6 @@
         r.win[m, z, y] = r.acc[q // 2, q % 2, 0:96, 0:512].astype(BF)
         q = 2 * m + 1
         r.dg[m, 0:96, :] = r.acc[q // 2, q % 2, 0:96, 0:512].astype(BF)
-        ag_first(r.dg.at[m, pl.ds(0, 96)], w_slot(m), w_ss(m), w_rs(m))
 
     @pl.when(c == y)
     def _():
@@ -688,14 +701,19 @@
             r.wout[m, z1] = r.acc[m // 2, m % 2, 96:224, 0:D].astype(BF)
 
     xf = s + 2 - 4 * x
+    for src, slot, ss, rs in att_sets:
+        ag_z0(slot, ss, rs)
     got(r.nall.at[xf], r.x_r.at[1])
     send(r.nall.at[xf], r.nall.at[xf], r.x_s.at[2], r.x_r.at[2], core)
-    for src, slot, ss, rs in att_sets:
-        ag_z0(slot, ss, rs)
+    for m in range(4):
+        ag_first(r.dg.at[m, pl.ds(0, 96)], w_slot(m), w_ss(m), w_rs(m))
     for src, slot, ss, rs in att_sets:
         ag_z1(slot, ss, rs)
-    tok_own(r.cota, 0)
-    for src, slot, ss, rs in att_sets[:2]:
+    tok_own(sel_slot, 2)
+    tok_own(cot_slot, 0)
+    ag_first(*ow_set)
+    ag_own(*ow_set[1:])
+    for src, slot, ss, rs in att_sets:
         ag_fin(slot, rs)
 
     def w_own(m):
@@ -735,8 +753,8 @@
             for k in range(3):
                 sent(r.wout.at[m, 0], r.o_s.at[m, k])
 
-    for m in range(4):
-        w_own(m)
+    w_own(0)
+    w_own(1)
 
     rows = jnp.zeros((8, D), F32)
     for k in range(8):
@@ -768,19 +786,25 @@
         cosv = r.cos_in[at, :]
         sinv = r.sin_in[at, :]
         for h in range(3):
-            g = pr[:, 128 * h : 128 * h + 128]
+            hc = 128 * h + 128 * (h // 2)
+            g = pr[:, hc : hc + 128]
             g = (g * cosv + swap_halves(g) * sinv).astype(BF).astype(F32)
             g = jnp.where(lane128 < 64, g * 0.125, g)
             r.kq[h, at, :] = pltpu.roll(g, 64, 1).astype(BF)
-        r.val[0, at, :] = pr[:, 384:512].astype(BF)
+        r.val[0, at, :] = pr[:, 256:384].astype(BF)
         r.val[1, at, :] = pr[:, 512:640].astype(BF)
         return carry
 
     lax.fori_loop(0, 4, project, 0)
 
+    ag_z0(*ow_set[1:])
+    w_own(2)
+    w_own(3)
     for m in range(4):
         w_relay(m)
-    tok_relay(r.cota, 0)
+    ag_z1(*ow_set[1:])
+    tok_near(sel_slot, 2)
+    tok_near(cot_slot, 0)
 
     for i in range(3, -1, -1):
         n = (i + 1) * TOK
@@ -810,17 +834,19 @@
         def _(i=i):
             r.arow[i] = r.att[i]
 
-        if i == 3:
+        if i == 1:
             ag_fin(o_slot, o_rs)
             send(r.ow.at[:, :, c], r.ow.at[:, :, c], r.ow_s.at[0], r.ow_r.at[0], core)
         if i == 2:
             w_relay_far(0)
+            tok_far(sel_slot, 2)
+            tok_far(cot_slot, 0)
         if i == 0:
             w_relay_far(1)
 
     got(r.ow.at[:, :, oc], r.ow_r.at[0])
     sent(r.ow.at[:, :, c], r.ow_s.at[0])
-    for src, slot, ss, rs in att_sets:
+    for src, slot, ss, rs in att_sets + (ow_set,):
         ag_sent(src, slot, ss)
     for i in range(4):
 
@@ -836,31 +862,23 @@
     r.mid[...] = mid
     r2 = lax.rsqrt(jnp.mean(mid * mid, axis=-1, keepdims=True) + EPSILON)
     nb = (mid * r2 * r.mrow[4:5, :]).astype(BF)
-    r.nown[...] = nb
     r.nta[jme, c, :, 0:D] = nb
-    r.nta[jme, c, :, D : D + 128] = r.sel_in[...]
-    tok_own(r.nta, 1)
-    tok_fin(r.cota, 0)
-    tok_relay(r.nta, 1)
-    tok_fin(r.nta, 1)
-
-    def gates(sel, nv):
+    tok_own(two_slot, 1)
+    tok_fin(sel_slot, 2)
+    tok_fin(cot_slot, 0)
+
+    def gates(nv):
         lg = nt(nv, r.rpad[...])
         lg = jnp.where(lane128 < 3, lg, -1e30)
         e = jnp.exp(lg - jnp.max(lg, axis=-1, keepdims=True))
         return e / jnp.sum(e, axis=-1, keepdims=True)
 
-    def route(g, carry):
-        j = lax.div(g, 2)
-        k = lax.rem(g, 2)
+    def route(j, k):
         sel = r.nta[j, k, :, D : D + 128].astype(F32)
-        pv = gates(sel, r.nta[j, k, :, 0:D])
-        r.gate[g] = jnp.where(lane128 < 3, pv * sel, sel)
-        r.acc[j, k] = jnp.zeros((TOK, D + 128), F32)
-        return carry
-
-    lax.fori_loop(0, 8, route, 0)
-    r.pown[...] = gates(None, r.nown[...])
+        pv = gates(r.nta[j, k, :, 0:D])
+        gv = jnp.where(lane128 < 3, pv * sel, jnp.where(lane128 == 3, sel, 0.0))
+        r.acc[j, k, :, 0:D] = jnp.zeros((TOK, D), F32)
+        r.acc[j, k, :, D : D + 128] = pltpu.roll(gv, 64, 1)
 
     def rs_first(m):
         send(r.win.at[m, :, oy], r.ry_in.at[m], r.rs_s.at[m, 0], r.rs_r.at[m, 0], yp)
@@ -868,6 +886,10 @@
         @pl.when(c != y)
         def _():
             send(r.gout.at[m], r.ry_out.at[m], r.rs_s.at[m, 1], r.rs_r.at[m, 1], yp)
+
+    def out_rows(m, k):
+        at = pl.ds(pl.multiple_of(128 * k, 128), 128)
+        return r.gs_out.at[at] if m == 3 else r.ge_out.at[m, at]
 
     def rs_y(m):
         got(r.ry_in.at[m], r.rs_r.at[m, 0])
@@ -889,8 +911,7 @@
         for k in range(2):
             zz = 2 * z1 + k
             r.win[m, zz, y] = (r.win[m, zz, y].astype(F32) + r.rz_in[m, k].astype(F32)).astype(BF)
-        send(r.win.at[m, zf, y], r.g_in.at[m, s, z0], r.rs_s.at[m, 4], r.rs_r.at[m, 4], z0p)
-        pltpu.make_async_copy(r.win.at[m, z, y], r.g_in.at[m, s, z0], r.loc.at[m, 0]).start()
+        send(r.win.at[m, zf, y], r.rzz.at[m], r.rs_s.at[m, 4], r.rs_r.at[m, 4], z0p)
 
         @pl.when(c == y)
         def _():
@@ -898,112 +919,185 @@
             v = (r.gout[m, z1].astype(F32) + r.rz_out[m].astype(F32)).astype(BF)
             r.gout[m, z1] = v
             g = r.gout.at[m, z1]
-            pltpu.make_async_copy(g, r.g_out.at[m, x], r.loc.at[m, 1]).start()
-            send(g, r.g_out.at[m, x], r.rs_s.at[m, 5], r.rs_r.at[m, 5], xp)
-            send(g, r.g_out.at[m, x], r.rs_s.at[m, 6], r.rs_r.at[m, 6], core)
+            pltpu.make_async_copy(g, out_rows(m, x), r.loc.at[m, 1]).start()
+            send(g, out_rows(m, x), r.rs_s.at[m, 5], r.rs_r.at[m, 5], xp)
+            send(g, out_rows(m, x), r.rs_s.at[m, 6], r.rs_r.at[m, 6], core)
+
+    def part(m, sx, sc):
+        return r.ga.at[2 * m + sx, pl.ds(0, 192), pl.ds(pl.multiple_of(512 * sc, 512), 512)]
 
     def rs_join(m):
-        got(r.g_in.at[m, s, 1 - z0], r.rs_r.at[m, 4])
-        pltpu.make_async_copy(r.win.at[m, z, y], r.g_in.at[m, s, z0], r.loc.at[m, 0]).wait()
-        g = r.g_in.at[m, s]
+        got(r.rzz.at[m], r.rs_r.at[m, 4])
+        cols = pl.ds(pl.multiple_of(512 * c, 512), 512)
+        mine = pl.ds(pl.multiple_of(96 * z0, 96), 96)
+        theirs = pl.ds(pl.multiple_of(96 - 96 * z0, 96), 96)
+        r.ga[2 * m + x, mine, cols] = r.win[m, z, y]
+        r.ga[2 * m + x, theirs, cols] = r.rzz[m]
+        g = part(m, x, c)
         send(g, g, r.rs_s.at[m, 7], r.rs_r.at[m, 7], xp)
         send(g, g, r.rs_s.at[m, 8], r.rs_r.at[m, 8], core)
 
     def rs_spread(m):
-        g = r.g_in.at[m, xf]
+        g = part(m, 1 - x, c)
         got(g, r.rs_r.at[m, 7])
         send(g, g, r.rs_s.at[m, 9], r.rs_r.at[m, 9], core)
 
         @pl.when(c == y)
         def _():
-            v = r.g_out.at[m, 1 - x]
+            v = out_rows(m, 1 - x)
             got(v, r.rs_r.at[m, 5])
             send(v, v, r.rs_s.at[m, 10], r.rs_r.at[m, 10], core)
 
     def rs_end(m):
-        got(r.g_in.at[m, s + 1 - 2 * c], r.rs_r.at[m, 8])
-        got(r.g_in.at[m, 3 - s], r.rs_r.at[m, 9])
+        got(part(m, x, oc), r.rs_r.at[m, 8])
+        got(part(m, 1 - x, oc), r.rs_r.at[m, 9])
+        for k in range(8):
+            h, kz, zz = k // 4, k // 2 % 2, k % 2
+            for q in range(4):
+                sc, sx = q // 2, q % 2
+                at = 512 * sc + 128 * (2 * h + kz)
+                v = r.ga[2 * m + sx, 96 * zz : 96 * zz + 96, at : at + 128]
+                if h == 0:
+                    r.ry_in[m, k, :, 128 * q : 128 * q + 128] = v
+                else:
+                    row = 96 * (k % 2)
+                    r.dg[2 * m + kz, row : row + 96, 128 * q : 128 * q + 128] = v
+            src = r.ry_in.at[m, k] if h == 0 else r.dg.at[2 * m + kz, pl.ds(96 * (k % 2), 96)]
+            dst = r.gs_in if m == 3 else r.ge_in.at[m]
+            pltpu.make_async_copy(src, dst.at[:, pl.ds(512 * k, 512)], r.fin.at[m, k]).start()
         sent(r.ry_in.at[m], r.rs_s.at[m, 0])
         sent(r.rz_in.at[m], r.rs_s.at[m, 2])
         sent(r.win.at[m, zf, y], r.rs_s.at[m, 4])
         for k in (7, 8, 9):
-            sent(r.g_in.at[m, s], r.rs_s.at[m, k])
+            sent(part(m, x, c), r.rs_s.at[m, k])
 
         @pl.when(c != y)
         def _():
             sent(r.gout.at[m], r.rs_s.at[m, 1])
-            got(r.g_out.at[m, x], r.rs_r.at[m, 6])
-            got(r.g_out.at[m, 1 - x], r.rs_r.at[m, 10])
+            got(out_rows(m, x), r.rs_r.at[m, 6])
+            got(out_rows(m, 1 - x), r.rs_r.at[m, 10])
 
         @pl.when(c == y)
         def _():
             g = r.gout.at[m, z1]
-            pltpu.make_async_copy(g, r.g_out.at[m, x], r.loc.at[m, 1]).wait()
+            pltpu.make_async_copy(g, out_rows(m, x), r.loc.at[m, 1]).wait()
             for k in (3, 5, 6, 10):
                 sent(g, r.rs_s.at[m, k])
 
-    def feed(m, carry):
-        @pl.when(m < 2)
-        def _():
-            w_relay_far(m + 2)
-
-        w_fin(m)
-
-        def tokens(g, inner):
-            j = lax.div(g, 2)
-            k = lax.rem(g, 2)
-            w = r.win[m].reshape(D, 512)
-            wo = r.wout[m].reshape(256, D)
-            gu = nn(r.nta[j, k, :, 0:D], w)
-            zv = gu[:, 0:256]
-            uv = gu[:, 256:512]
-            sg = 1.0 / (1.0 + jnp.exp(-zv))
-            sw = zv * sg
-            act = (sw * uv).astype(BF).astype(F32)
-            dr = nt(r.cota[j, k], wo)
-            gv = jnp.sum(jnp.where(lane128 == m, r.gate[g], 0.0), axis=-1, keepdims=True)
-            gg = jnp.sum(act * dr, axis=-1, keepdims=True)
-            r.ga[g, :, pl.ds(pl.multiple_of(m * 256, 256), 256)] = (act * gv).astype(BF)
-            d = dr * gv
-            dg = jnp.concatenate([d * uv * (sg * (1.0 + zv * (1.0 - sg))), d * sw], axis=1).astype(BF)
-            r.dg[g] = dg
-            r.acc[j, k, :, 0:D] += nt(dg, w)
-            r.acc[j, k, :, D : D + 128] += jnp.where(lane128 == m, gg, 0.0)
-            return inner
-
-        lax.fori_loop(0, 8, tokens, 0)
+    def rs_done(m):
+        for k in range(8):
+            dst = r.gs_in if m == 3 else r.ge_in.at[m]
+            piece = dst.at[:, pl.ds(512 * k, 512)]
+            pltpu.make_async_copy(piece, piece, r.fin.at[m, k]).wait()
+
+    def tokens(m, j, k):
+        g = 2 * j + k
+        w = r.win[m].reshape(D, 512)
+        wo = r.wout[m].reshape(256, D)
+        gu = nn(r.nta[j, k, :, 0:D], w)
+        zv = gu[:, 0:256]
+        uv = gu[:, 256:512]
+        sg = 1.0 / (1.0 + jnp.exp(-zv))
+        sw = zv * sg
+        act = (sw * uv).astype(BF).astype(F32)
+        dr = nt(r.cota[j, k], wo)
+        side = r.acc[j, k, :, D : D + 128]
+        gv = jnp.sum(jnp.where(lane128 == m + 64, side, 0.0), axis=-1, keepdims=True)
+        gg = jnp.sum(act * dr, axis=-1, keepdims=True)
+        r.ga[g, :, pl.ds(pl.multiple_of(m * 256, 256), 256)] = (act * gv).astype(BF)
+        d = dr * gv
+        dg = jnp.concatenate([d * uv * (sg * (1.0 + zv * (1.0 - sg))), d * sw], axis=1).astype(BF)
+        r.dg[g] = dg
+        r.acc[j, k, :, 0:D] += nt(dg, w)
+        r.acc[j, k, :, D : D + 128] = side + jnp.where(lane128 == m, gg, 0.0)
+
+    def weight_grads(m):
         nta = r.nta[:, :, :, 0:D].reshape(2048, D)
         r.win[m] = tn(nta, r.dg[...].reshape(2048, 512)).astype(BF).reshape(4, 2, 96, 512)
         gam = r.ga[:, :, pl.ds(pl.multiple_of(m * 256, 256), 256)].reshape(2048, 256)
         r.gout[m] = tn(gam, r.cota[...].reshape(2048, D)).astype(BF).reshape(2, 128, D)
         rs_first(m)
 
-        @pl.when(m >= 1)
-        def _():
-            rs_y(m - 1)
-
-        @pl.when(m >= 2)
-        def _():
-            rs_z(m - 2)
-
-        return carry
-
+    def pack(j, k):
+        r.ngb[j, k, :, 0:D] = r.acc[j, k, :, 0:D].astype(BF)
+        v = jnp.where(lane128 < 64, r.acc[j, k, :, D : D + 128], 0.0)
+        hi = v.astype(BF).astype(F32)
+        r.ngb[j, k, :, D : D + 128] = (hi + pltpu.roll(v - hi, 64, 1)).astype(BF)
+
+    w_fin(0)
     for m in range(4):
         sent(r.dg.at[m, pl.ds(0, 96)], r.w_s.at[m, 0])
-    lax.fori_loop(0, 4, feed, 0)
-
-    def pack(g, carry):
-        j = lax.div(g, 2)
-        k = lax.rem(g, 2)
-        r.nta[j, k, :, 0:D] = r.acc[j, k, :, 0:D].astype(BF)
-        v = r.acc[j, k, :, D : D + 128]
-        hi = v.astype(BF).astype(F32)
-        r.nta[j, k, :, D : D + 128] = (hi + pltpu.roll(v - hi, 64, 1)).astype(BF)
+
+    def arrive(p, carry):
+        q = lax.div(p, 2)
+        k2 = lax.rem(p, 2)
+        j = block_at(q)
+        k = c + k2 * (1 - 2 * c)
+
+        @pl.when(p == 2)
+        def _():
+            tok_near(two_slot, 1)
+
+        @pl.when(k2 == 1)
+        def _():
+            got(two_slot(j, k), r.tok_r.at[1, p])
+
+        @pl.when(p == 4)
+        def _():
+            w_relay_far(2)
+
+        @pl.when(p == 5)
+        def _():
+            tok_far(two_slot, 1)
+
+        route(j, k)
+        tokens(0, j, k)
         return carry
 
-    lax.fori_loop(0, 8, pack, 0)
-    sum_first(r.nta, r.ng_c, 0)
-    sum_core(r.nta, r.ng_c, r.ng_p, 0)
+    lax.fori_loop(0, 8, arrive, 0)
+    weight_grads(0)
+    tok_sent(two_slot, 1)
+    tok_sent(sel_slot, 2)
+    tok_sent(cot_slot, 0)
+
+    def feed(m, carry):
+        @pl.when(m == 1)
+        def _():
+            w_relay_far(3)
+
+        w_fin(m)
+
+        def each(p, inner):
+            k2 = lax.div(p, 4)
+            k = oc + k2 * (2 * c - 1)
+            j = block_at(3 - lax.rem(p, 4))
+            tokens(m, j, k)
+
+            @pl.when(m == 3)
+            def _():
+                pack(j, k)
+
+            @pl.when((m == 3) & (p == 3))
+            def _():
+                sum_first(r.ngb, r.ng_c, 0)
+
+            return inner
+
+        lax.fori_loop(0, 8, each, 0)
+
+        @pl.when(m == 2)
+        def _():
+            rs_y(0)
+
+        @pl.when(m == 3)
+        def _():
+            sum_core(r.ngb, r.ng_c, r.ng_p, 0)
+            rs_y(1)
+
+        weight_grads(m)
+        return carry
+
+    lax.fori_loop(1, 4, feed, 0)
 
     def mix(g, carry):
         j = lax.div(g, 2)
@@ -1012,21 +1106,37 @@
         return carry
 
     lax.fori_loop(0, 4, mix, 0)
-    sum_relay(r.nta, r.ng_p, 0)
+    sum_relay(r.ngb, r.ng_p, 0)
     lax.fori_loop(4, 8, mix, 0)
-    rs_y(3)
-    ngs = sum_fin(r.nta, r.ng_c, r.ng_p, 0)
-    sum_first(r.cota, r.out_c, 1)
+    rs_y(2)
+    out_c = r.ng_c.at[:, :, pl.ds(0, D)]
+    out_p = r.ng_p.at[:, :, pl.ds(0, D)]
+    ngs = sum_fin(r.ngb, r.ng_c, r.ng_p, 0)
+    rs_z(0)
+
+    small_dev = (core, xp, yp, z1p, z0p)
+
+    def small_send(k):
+        r.small_o[k] = r.small[...]
+        send(r.small_o.at[k], r.small_i.at[k], r.sm_s.at[k], r.sm_r.at[k], small_dev[k])
+
+    def small_add(k):
+        got(r.small_i.at[k], r.sm_r.at[k])
+        r.small[...] += r.small_i[k]
+        sent(r.small_o.at[k], r.sm_s.at[k])
+        if k < 4:
+            small_send(k + 1)
 
     upstream = r.cot_in[...].astype(F32)
     mid = r.mid[...]
     r2 = lax.rsqrt(jnp.mean(mid * mid, axis=-1, keepdims=True) + EPSILON)
     gg = ngs[:, D : D + 128]
     gg = gg + pltpu.roll(gg, 64, 1)
-    pv = r.pown[...]
+    nown = r.nta[jme, c, :, 0:D]
+    pv = gates(nown)
     pg = jnp.where(lane128 < 3, gg * r.sel_in[...].astype(F32), 0.0)
     lg = (pv * (pg - jnp.sum(pv * pg, axis=-1, keepdims=True))).astype(BF)
-    rgrad = tn(lg, r.nown[...])
+    rgrad = tn(lg, nown)
     ng = ngs[:, 0:D] + nn(lg, r.rpad[...])
     gain2 = r.mrow[4:5, :]
     fgain = jnp.sum(ng * mid * r2, axis=0, keepdims=True)
@@ -1049,13 +1159,19 @@
         def _(i=i):
             r.dat[i] = r.att[i]
 
+    small_send(0)
     for i in range(4):
         og = tn(r.arow[i][:, 0:192], ml).astype(BF)
         og = og.reshape(2, 2, 48, D)
         for k in range(2):
             r.og[k, i] = og[:, :, :, 384 * k : 384 * k + 384]
     send(r.og.at[oc], r.og_c, r.og_s.at[0], r.og_r.at[0], core)
-    sum_core(r.cota, r.out_c, r.out_p, 1)
+    for i in range(4):
+        r.acc[i, 0, :, 0:QKV_PAD] = jnp.zeros((TOK, QKV_PAD), F32)
+        r.acc[i, 1, :, 0:D] = jnp.zeros((TOK, D), F32)
+    small_add(0)
+    rs_y(3)
+    rs_z(1)
     for i in range(4):
 
         @pl.when(s != i)
@@ -1063,19 +1179,97 @@
             got(r.dat.at[i], r.d_r.at[i])
             sent(r.att.at[i], r.d_s.at[i])
 
-    rs_z(2)
-
-    for i in range(4):
-        r.acc[i, 0, :, 0:QKV_PAD] = jnp.zeros((TOK, QKV_PAD), F32)
-    for i in range(3, -1, -1):
-        base = i * (i + 1) // 2
-
-        def heads_back(h, carry, i=i, base=base):
-            hv = lax.div(h, 2)
-            here = lax.div(lane128, 64) == lax.rem(h, 2)
-            vat = pl.ds(pl.multiple_of(hv * 128, 128), 128)
-            cat = pl.ds(pl.multiple_of(384 + hv * 128, 128), 128)
-            hat = pl.ds(pl.multiple_of(h * 128, 128), 128)
+    sum_first(r.cota, out_c, 1)
+
+    chunks = ((0, 128), (128, 256), (384, 256))
+
+    def q_first(n):
+        at = pl.ds(chunks[n][0], chunks[n][1])
+        send(r.wq.at[:, oy, :, at], r.q_y.at[:, :, at], r.q_s.at[n, 0], r.q_r.at[n, 0], yp)
+
+    def q_add_y(n):
+        a, e = chunks[n][0], chunks[n][0] + chunks[n][1]
+        at = pl.ds(a, e - a)
+        got(r.q_y.at[:, :, at], r.q_r.at[n, 0])
+        for k in range(4):
+            v = r.wq[k, y, :, a:e].astype(F32) + r.q_y[k, :, a:e].astype(F32)
+            r.wq[k, y, :, a:e] = v.astype(BF)
+        send(
+            r.wq.at[pl.ds(2 - 2 * z1, 2), y, :, at],
+            r.q_z.at[:, :, at],
+            r.q_s.at[n, 1],
+            r.q_r.at[n, 1],
+            z1p,
+        )
+
+    def q_add_z(n):
+        a, e = chunks[n][0], chunks[n][0] + chunks[n][1]
+        at = pl.ds(a, e - a)
+        got(r.q_z.at[:, :, at], r.q_r.at[n, 1])
+        for k in range(2):
+            v = r.wq[2 * z1 + k, y, :, a:e].astype(F32) + r.q_z[k, :, a:e].astype(F32)
+            r.wq[2 * z1 + k, y, :, a:e] = v.astype(BF)
+        send(r.wq.at[zf, y, :, at], r.q_w.at[:, at], r.q_s.at[n, 2], r.q_r.at[n, 2], z0p)
+
+    def head_ends(a, w):
+        at = pl.ds(a, w)
+        for i in range(4):
+            for k in range(0, w, 128):
+                g = r.acc[i, 0, :, a + k : a + k + 128].astype(BF)
+                if a + k in (0, 128, 384):
+                    g = g.astype(F32)
+                    cosv = r.cos_in[i * TOK : i * TOK + TOK, :]
+                    sinv = r.sin_in[i * TOK : i * TOK + TOK, :]
+                    g = (g * cosv - swap_halves(g) * sinv).astype(BF)
+                r.nta[i, 0, :, a + k : a + k + 128] = g
+        wc = r.wq[:, :, :, a : a + w].reshape(D, w)
+        for i in range(4):
+            r.acc[i, 1, :, 0:D] += nt(r.nta[i, 0, :, a : a + w], wc)
+        pg = r.nta[:, 0, :, a : a + w].reshape(1024, w)
+        wg = tn(r.nall[...].reshape(1024, D), pg)
+        r.wq[:, :, :, a : a + w] = wg.astype(BF).reshape(4, 2, 96, w)
+
+    def og_core():
+        got(r.og_c, r.og_r.at[0])
+        for k in range(4):
+            r.og[c, k] = (r.og[c, k].astype(F32) + r.og_c[k].astype(F32)).astype(BF)
+        send(r.og.at[c, :, :, 1 - x], r.og_x, r.og_s.at[1], r.og_r.at[1], xp)
+
+    def og_xp():
+        got(r.og_x, r.og_r.at[1])
+        for k in range(4):
+            r.og[c, k, :, x] = (r.og[c, k, :, x].astype(F32) + r.og_x[k].astype(F32)).astype(BF)
+        send(r.og.at[c, :, oy, x], r.og_y, r.og_s.at[2], r.og_r.at[2], yp)
+
+    def og_yp():
+        got(r.og_y, r.og_r.at[2])
+        for k in range(4):
+            r.og[c, k, y, x] = (r.og[c, k, y, x].astype(F32) + r.og_y[k].astype(F32)).astype(BF)
+        send(r.og.at[c, pl.ds(2 - 2 * z1, 2), y, x], r.og_z, r.og_s.at[3], r.og_r.at[3], z1p)
+
+    def og_z1p():
+        got(r.og_z, r.og_r.at[3])
+        for k in range(2):
+            v = r.og[c, 2 * z1 + k, y, x].astype(F32) + r.og_z[k].astype(F32)
+            r.og[c, 2 * z1 + k, y, x] = v.astype(BF)
+        send(r.og.at[c, zf, y, x], r.og_w, r.og_s.at[4], r.og_r.at[4], z0p)
+
+    def og_z0p():
+        got(r.og_w, r.og_r.at[4])
+        r.og[c, z, y, x] = (r.og[c, z, y, x].astype(F32) + r.og_w[...].astype(F32)).astype(BF)
+        ogf = r.og.at[c, z, y, x]
+        r.g_ow[s] = r.og[c, z, y, x]
+        send(ogf, r.g_ow.at[s], r.og_s.at[6], r.og_r.at[6], xp)
+        send(ogf, r.g_ow.at[s], r.og_s.at[5], r.og_r.at[5], core)
+
+    def heads_back(h, carry):
+        hv = lax.div(h, 2)
+        here = lax.div(lane128, 64) == lax.rem(h, 2)
+        vat = pl.ds(pl.multiple_of(hv * 128, 128), 128)
+        cat = pl.ds(pl.multiple_of(256 + hv * 256, 128), 128)
+        hat = pl.ds(pl.multiple_of(h * 128 + hv * 128, 128), 128)
+        for i in range(3, -1, -1):
+            base = i * (i + 1) // 2
             da = jnp.where(here, r.dat[i, :, vat].astype(F32), 0.0).astype(BF)
             kqi = r.kq[h, i * TOK : i * TOK + TOK, :].astype(F32)
             qi = jnp.where(lane128 >= 64, kqi, 0.0).astype(BF)
@@ -1091,124 +1285,103 @@
                 r.acc[j, 0, :, hat] += tn(ds, qi)
                 r.acc[j, 0, :, cat] += tn(pf[j], da)
             r.acc[i, 0, :, hat] += jnp.where(lane128 < 64, dq * 0.125, 0.0)
-            return carry
-
-        lax.fori_loop(0, 3, heads_back, 0)
-        cosv = r.cos_in[i * TOK : i * TOK + TOK, :]
-        sinv = r.sin_in[i * TOK : i * TOK + TOK, :]
-        for h in range(3):
-            g = r.acc[i, 0, :, 128 * h : 128 * h + 128].astype(BF).astype(F32)
-            r.nta[i, 0, :, 128 * h : 128 * h + 128] = (g * cosv - swap_halves(g) * sinv).astype(BF)
-        r.nta[i, 0, :, 384:640] = r.acc[i, 0, :, 384:640].astype(BF)
-        r.ng1[i // 2, i % 2] = nt(r.nta[i, 0, :, 0:QKV_PAD], r.wq[...].reshape(D, QKV_PAD)).astype(BF)
-        if i == 3:
-            rs_z(3)
-            got(r.og_c, r.og_r.at[0])
-            for k in range(4):
-                r.og[c, k] = (r.og[c, k].astype(F32) + r.og_c[k].astype(F32)).astype(BF)
-            send(r.og.at[c, :, :, 1 - x], r.og_x, r.og_s.at[1], r.og_r.at[1], xp)
-            sum_relay(r.cota, r.out_p, 1)
-        if i == 2:
+
+        @pl.when(h == 0)
+        def _():
+            head_ends(*chunks[0])
+            q_first(0)
+            og_core()
             rs_join(0)
+            sum_core(r.cota, out_c, out_p, 1)
+            rs_z(2)
+            small_add(1)
+
+        @pl.when(h == 1)
+        def _():
+            head_ends(*chunks[1])
+            q_first(1)
+            og_xp()
+            sum_relay(r.cota, out_p, 1)
+            q_add_y(0)
             rs_join(1)
-            got(r.og_x, r.og_r.at[1])
-            for k in range(4):
-                r.og[c, k, :, x] = (r.og[c, k, :, x].astype(F32) + r.og_x[k].astype(F32)).astype(BF)
-            send(r.og.at[c, :, oy, x], r.og_y, r.og_s.at[2], r.og_r.at[2], yp)
-            tot = sum_fin(r.cota, r.out_c, r.out_p, 1)
-            r.out[...] = (r.mid[...] + tot).astype(BF)
-        if i == 1:
-            rs_join(2)
             rs_spread(0)
-            got(r.og_y, r.og_r.at[2])
-            for k in range(4):
-                r.og[c, k, y, x] = (r.og[c, k, y, x].astype(F32) + r.og_y[k].astype(F32)).astype(BF)
-            send(r.og.at[c, pl.ds(2 - 2 * z1, 2), y, x], r.og_z, r.og_s.at[3], r.og_r.at[3], z1p)
-
-    ng1_c = r.ng_c.at[pl.ds(0, 2), :, pl.ds(0, D)]
-    ng1_x = r.ng_p.at[0, :, pl.ds(0, D)]
-    send(r.ng1.at[:, oc], ng1_c, r.n_s.at[0], r.n_r.at[0], core)
-    wg = tn(r.nall[...].reshape(1024, D), r.nta[:, 0, :, 0:QKV_PAD].reshape(1024, QKV_PAD))
-    r.wq[...] = wg.astype(BF).reshape(4, 2, 96, QKV_PAD)
-    send(r.wq.at[:, oy], r.q_y, r.q_s.at[0], r.q_r.at[0], yp)
-    got(ng1_c, r.n_r.at[0])
+            small_add(2)
+
+        @pl.when(h == 2)
+        def _():
+            head_ends(*chunks[2])
+            q_first(2)
+
+        return carry
+
+    lax.fori_loop(0, 3, heads_back, 0)
+
+    n_slot = lambda i: r.nta.at[i, 1, :, pl.ds(0, D)]
+    for i in range(4):
+        r.nta[i, 1, :, 0:D] = r.acc[i, 1, :, 0:D].astype(BF)
     for k in range(2):
-        r.ng1[k, c] = (r.ng1[k, c].astype(F32) + r.ng_c[k, :, 0:D].astype(F32)).astype(BF)
-    send(r.ng1.at[1 - x, c], ng1_x, r.n_s.at[1], r.n_r.at[1], xp)
+        send(n_slot(2 * k + oc), r.n_c.at[k], r.n_s.at[k], r.n_r.at[k], core)
+    og_yp()
+    q_add_y(1)
+    for k in range(2):
+        got(r.n_c.at[k], r.n_r.at[k])
+        v = r.nta[2 * k + c, 1, :, 0:D].astype(F32) + r.n_c[k].astype(F32)
+        r.nta[2 * k + c, 1, :, 0:D] = v.astype(BF)
+    send(n_slot(2 - 2 * x + c), r.n_x, r.n_s.at[2], r.n_r.at[2], xp)
+    q_add_z(0)
+    rs_z(3)
+    rs_join(2)
+    rs_spread(1)
+    rs_end(0)
+    small_add(3)
+    q_add_y(2)
+    og_z1p()
+    q_add_z(1)
     rs_join(3)
-    for k in range(1, 3):
-        rs_spread(k)
-    got(r.og_z, r.og_r.at[3])
-    for k in range(2):
-        v = r.og[c, 2 * z1 + k, y, x].astype(F32) + r.og_z[k].astype(F32)
-        r.og[c, 2 * z1 + k, y, x] = v.astype(BF)
-    send(r.og.at[c, zf, y, x], r.og_w, r.og_s.at[4], r.og_r.at[4], z0p)
-
-    got(ng1_x, r.n_r.at[1])
-    sent(r.ng1.at[:, oc], r.n_s.at[0])
-    sent(r.ng1.at[1 - x, c], r.n_s.at[1])
-    ng = r.ng1[x, c].astype(F32) + r.ng_p[0, :, 0:D].astype(F32)
+    rs_spread(2)
+    tot = sum_fin(r.cota, out_c, out_p, 1)
+    r.out[...] = (r.mid[...] + tot).astype(BF)
+    rs_end(1)
+    small_add(4)
+    r.g_small[...] = r.small[...]
+    og_z0p()
+
+    got(r.n_x, r.n_r.at[2])
+    for k in range(3):
+        sent(r.n_x, r.n_s.at[k])
+    ng = r.nta[s, 1, :, 0:D].astype(F32) + r.n_x[...].astype(F32)
     xv = r.x_in[...].astype(F32)
     r1 = lax.rsqrt(jnp.mean(xv * xv, axis=-1, keepdims=True) + EPSILON)
-    gain1 = r.mrow[3:4, :]
-    again = jnp.sum(ng * xv * r1, axis=0, keepdims=True)
-    sc = ng * gain1
+    sc = ng * r.mrow[3:4, :]
     r.igrad[...] = (
         r.igrad[...] + r1 * sc - xv * (r1 * r1 * r1) * jnp.mean(sc * xv, axis=-1, keepdims=True)
     )
-    r.small[...] += jnp.where(row8 == 3, again, 0.0)
-
-    def pair_sum(k, dev):
-        r.small_o[k] = r.small[...]
-        send(r.small_o.at[k], r.small_i.at[k], r.sm_s.at[k], r.sm_r.at[k], dev)
-
-    def pair_add(k):
-        got(r.small_i.at[k], r.sm_r.at[k])
-        r.small[...] += r.small_i[k]
-        sent(r.small_o.at[k], r.sm_s.at[k])
-
-    pair_sum(0, core)
-    got(r.q_y, r.q_r.at[0])
-    for k in range(4):
-        r.wq[k, y] = (r.wq[k, y].astype(F32) + r.q_y[k].astype(F32)).astype(BF)
-    send(r.wq.at[pl.ds(2 - 2 * z1, 2), y], r.q_z, r.q_s.at[1], r.q_r.at[1], z1p)
-    pair_add(0)
-    pair_sum(1, xp)
-    got(r.og_w, r.og_r.at[4])
-    r.og[c, z, y, x] = (r.og[c, z, y, x].astype(F32) + r.og_w[...].astype(F32)).astype(BF)
-    ogf = r.og.at[c, z, y, x]
-    r.g_ow[s] = r.og[c, z, y, x]
-    send(ogf, r.g_ow.at[s], r.og_s.at[5], r.og_r.at[5], core)
-    send(ogf, r.g_ow.at[s], r.og_s.at[6], r.og_r.at[6], xp)
-    pair_add(1)
-    pair_sum(2, yp)
+    q_add_z(2)
     rs_spread(3)
-    got(r.q_z, r.q_r.at[1])
-    for k in range(2):
-        v = r.wq[2 * z1 + k, y].astype(F32) + r.q_z[k].astype(F32)
-        r.wq[2 * z1 + k, y] = v.astype(BF)
-    send(r.wq.at[zf, y], r.q_w, r.q_s.at[2], r.q_r.at[2], z0p)
-    pair_add(2)
-    pair_sum(3, z1p)
+    rs_end(2)
     got(r.g_ow.at[xf], r.og_r.at[6])
     send(r.g_ow.at[xf], r.g_ow.at[xf], r.og_s.at[7], r.og_r.at[7], core)
-    got(r.q_w, r.q_r.at[2])
-    r.wq[z, y] = (r.wq[z, y].astype(F32) + r.q_w[...].astype(F32)).astype(BF)
-    r.g_q[s] = r.wq[z, y]
-    send(r.wq.at[z, y], r.g_q.at[s], r.q_s.at[3], r.q_r.at[3], xp)
-    send(r.wq.at[z, y], r.g_q.at[s], r.q_s.at[4], r.q_r.at[4], core)
-    pair_add(3)
-    pair_sum(4, z0p)
-    for m in range(4):
-        rs_end(m)
-    got(r.g_q.at[xf], r.q_r.at[3])
-    send(r.g_q.at[xf], r.g_q.at[xf], r.q_s.at[5], r.q_r.at[5], core)
-    pair_add(4)
-    r.g_small[...] = r.small[...]
+
+    for n in range(3):
+        got(r.q_w.at[:, pl.ds(*chunks[n])], r.q_r.at[n, 2])
+    qf = r.wq[z, y].astype(F32) + r.q_w[...].astype(F32)
+    qf = jnp.concatenate([qf, jnp.zeros((32, QKV_PAD), F32)], axis=0)
+    qt = jnp.transpose(qf).astype(BF)
+    for k, at in enumerate((0, 64, 256, 128, 192, 320, 384, 448, 512)):
+        r.g_q[s, 64 * k : 64 * k + 64, :] = qt[at : at + 64, :]
+    g = r.g_q.at[s]
+    send(g, g, r.qg_s.at[0], r.qg_r.at[0], xp)
+    send(g, g, r.qg_s.at[1], r.qg_r.at[1], core)
+    rs_end(3)
+    got(r.g_q.at[xf], r.qg_r.at[0])
+    send(r.g_q.at[xf], r.g_q.at[xf], r.qg_s.at[2], r.qg_r.at[2], core)
     got(r.g_ow.at[s + 1 - 2 * c], r.og_r.at[5])
     got(r.g_ow.at[3 - s], r.og_r.at[7])
-    got(r.g_q.at[s + 1 - 2 * c], r.q_r.at[4])
-    got(r.g_q.at[3 - s], r.q_r.at[5])
+    for n in range(3):
+        at = pl.ds(*chunks[n])
+        sent(r.q_y.at[:, :, at], r.q_s.at[n, 0])
+        sent(r.q_z.at[:, :, at], r.q_s.at[n, 1])
+        sent(r.q_w.at[:, at], r.q_s.at[n, 2])
     sent(r.og_c, r.og_s.at[0])
     sent(r.og_x, r.og_s.at[1])
     sent(r.og_y, r.og_s.at[2])
@@ -1216,10 +1389,12 @@
     sent(r.og_w, r.og_s.at[4])
     for k in (5, 6, 7):
         sent(r.g_ow.at[0], r.og_s.at[k])
-    sent(r.q_y, r.q_s.at[0])
-    sent(r.q_z, r.q_s.at[1])
-    for k in (2, 3, 4, 5):
-        sent(r.q_w, r.q_s.at[k])
+    for m in range(4):
+        rs_done(m)
+    got(r.g_q.at[s + 1 - 2 * c], r.qg_r.at[1])
+    got(r.g_q.at[3 - s], r.qg_r.at[2])
+    for k in range(3):
+        sent(g, r.qg_s.at[k])
 
 
 def vmem(shape, kind=BF):
@@ -1232,15 +1407,18 @@
         ["x_in", "cot_in", "wq_in", "misc_in", "ow_in", "sel_in", "cos_in", "sin_in"]
         + ["e_in", "e_out", "s_in", "s_out"]
     )
-    out_names = ["out", "igrad", "g_small", "g_q", "g_ow", "g_in", "g_out"]
+    out_names = ["out", "igrad", "g_small", "g_q", "g_ow"]
+    out_names += ["ge_in", "gs_in", "ge_out", "gs_out"]
     out_shapes = (
         ((TOK, D), BF),
         ((TOK, D), F32),
         ((8, D), F32),
-        ((4, 96, QKV_PAD), BF),
+        ((4, 576, 128), BF),
         ((4, 48, 384), BF),
-        ((4, 4, 2, 96, 512), BF),
-        ((4, 2, 128, D), BF),
+        ((3, 96, 4096), BF),
+        ((96, 4096), BF),
+        ((3, 256, D), BF),
+        ((256, D), BF),
     )
     scratch = {
         "nall": vmem((4, TOK, D)),
@@ -1254,13 +1432,10 @@
         "arow": vmem((4, TOK, 256)),
         "dat": vmem((4, TOK, 256)),
         "mid": vmem((TOK, D), F32),
-        "nown": vmem((TOK, D)),
-        "pown": vmem((TOK, 128), F32),
         "mrow": vmem((8, D), F32),
         "rpad": vmem((128, D)),
         "nta": vmem((4, 2, TOK, D + 128)),
         "cota": vmem((4, 2, TOK, D)),
-        "gate": vmem((8, TOK, 128), F32),
         "win": vmem((4, 4, 2, 96, 512)),
         "wout": vmem((4, 2, 128, D)),
         "dg": vmem((8, TOK, 512)),
@@ -1269,13 +1444,14 @@
         "gout": vmem((4, 2, 128, D)),
         "ry_in": vmem((4, 4, 96, 512)),
         "ry_out": vmem((4, 2, 128, D)),
+        "rzz": vmem((4, 96, 512)),
         "rz_in": vmem((4, 2, 96, 512)),
         "rz_out": vmem((4, 128, D)),
         "ng_c": vmem((4, TOK, D + 128)),
         "ng_p": vmem((3, TOK, D + 128)),
-        "out_c": vmem((4, TOK, D)),
-        "out_p": vmem((3, TOK, D)),
-        "ng1": vmem((2, 2, TOK, D)),
+        "ngb": vmem((4, 2, TOK, D + 128)),
+        "n_c": vmem((2, TOK, D)),
+        "n_x": vmem((TOK, D)),
         "og": vmem((2, 4, 2, 2, 48, 384)),
         "og_c": vmem((4, 2, 2, 48, 384)),
         "og_x": vmem((4, 2, 48, 384)),
@@ -1299,8 +1475,8 @@
         "ow_r": dma((1,)),
         "x_s": dma((3,)),
         "x_r": dma((3,)),
-        "tok_s": dma((2, 7)),
-        "tok_r": dma((2, 7)),
+        "tok_s": dma((3, 7)),
+        "tok_r": dma((3, 8)),
         "a_s": dma((4,)),
         "a_r": dma((4,)),
         "d_s": dma((4,)),
@@ -1312,10 +1488,13 @@
         "loc": dma((4, 2)),
         "og_s": dma((8,)),
         "og_r": dma((8,)),
-        "q_s": dma((6,)),
-        "q_r": dma((6,)),
-        "n_s": dma((2,)),
-        "n_r": dma((2,)),
+        "q_s": dma((3, 3)),
+        "q_r": dma((3, 3)),
+        "qg_s": dma((3,)),
+        "qg_r": dma((3,)),
+        "fin": dma((4, 8)),
+        "n_s": dma((3,)),
+        "n_r": dma((3,)),
         "sm_s": dma((5,)),
         "sm_r": dma((5,)),
     }
@@ -1326,7 +1505,7 @@
         functools.partial(layer_kernel, names),
         out_shape=[jax.ShapeDtypeStruct(*one) for one in out_shapes],
         in_specs=[in_vmem] * 8 + [in_any] * 4,
-        out_specs=[in_vmem] * 5 + [in_any] * 2,
+        out_specs=[in_vmem] * 5 + [in_any] * 4,
         scratch_shapes=list(scratch.values()),
         compiler_params=pltpu.CompilerParams(
             collective_id=0, has_side_effects=True, vmem_limit_bytes=VMEM_LIMIT
@@ -1357,9 +1536,19 @@
     s = lax.axis_index("seq")
     c = s % 2
     mine = lax.dynamic_slice_in_dim(qkv_weight, 3 * s, 3, axis=1).astype(BF)
-    pairs = mine[:, :, 0:2].reshape(96, 384)
+    pairs = mine[:, :, 0:2].reshape(96, 3, 128)
     values = mine[:, :, 2].reshape(96, 192)
-    wq = jnp.concatenate([pairs, values, jnp.zeros((96, 64), BF)], axis=1)
+    wq = jnp.concatenate(
+        [
+            pairs[:, 0],
+            pairs[:, 1],
+            values[:, 0:128],
+            pairs[:, 2],
+            values[:, 128:192],
+            jnp.zeros((96, 64), BF),
+        ],
+        axis=1,
+    )
     misc = jnp.concatenate(
         [router_weight.T, attn_gain[None], ffn_gain[None], jnp.zeros((3, 96), F32)], axis=0
     )
@@ -1375,7 +1564,7 @@
     cos_table = jnp.asarray(np.tile(np.cos(angle), (1, 4)).astype(np.float32))
     sine = np.sin(angle)
     sin_table = jnp.asarray(np.tile(np.concatenate([-sine, sine], 1), (1, 2)).astype(np.float32))
-    out, igrad, small, g_q, g_ow, g_in, g_out = layer_call(
+    out, igrad, small, g_q, g_ow, ge_in, gs_in, ge_out, gs_out = layer_call(
         (
             inputs[0],
             cotangent[0],
@@ -1392,26 +1581,22 @@
         sin_table,
     )
     shard = lax.dynamic_slice_in_dim(small, 96 * b, 96, axis=1)
-    pairs = g_q[:, :, 0:384].reshape(4, 96, 3, 2, 64)
-    values = g_q[:, :, 384:576].reshape(4, 96, 3, 1, 64)
-    qkv_grad = jnp.concatenate([pairs, values], axis=3).transpose(1, 0, 2, 3, 4)
-    qkv_grad = qkv_grad.reshape(96, HEADS, 3, HEAD_DIM).astype(F32)
+    qkv_grad = g_q.reshape(HEADS, 3, HEAD_DIM, 128)[..., 0:96].transpose(3, 0, 1, 2).astype(F32)
+    gain_grad = jnp.sum(qkv_weight.astype(BF).astype(F32) * qkv_grad, axis=(1, 2, 3))
+    gain_grad = gain_grad / attn_gain.astype(BF).astype(F32)
     ow_grad = g_ow.reshape(2, 2, 48, 384).transpose(0, 2, 1, 3).reshape(96, D).astype(F32)
-    g = g_in.reshape(4, 2, 2, 2, 96, 2, 2, 128).transpose(0, 4, 5, 6, 3, 2, 1, 7)
-    g = g.reshape(4, 96, 2 * FF).astype(F32)
-    go = g_out.reshape(4, 256, D).astype(F32)
     return (
         out[None],
         igrad[None],
-        shard[3],
+        gain_grad,
         qkv_grad,
         ow_grad,
         shard[4],
         shard[0:3].T,
-        g[:3],
-        go[:3],
-        g[3],
-        go[3],
+        ge_in.astype(F32),
+        ge_out.astype(F32),
+        gs_in.astype(F32),
+        gs_out.astype(F32),
     )
 
 

time: 327 us -> 272 us (0.83)
  local copies, waits for them, and re-layouts: 41.3 us -> 7.69 us
  Pallas kernels: 280 us -> 251 us
  other arithmetic: 4.67 us -> 11.4 us
    pallas_call x1, Pallas kernels: 280 us -> 251 us  [layer_call(): pl.pallas_call(functools.partial(layer_kernel, names), out_shape=[jax.Sha...]
    slice x13 -> x5, local copies, waits for them, and re-layouts: 25 us -> 0.03 us  [the longest x2 0.02 us: fast_device(): pairs = mine[:, :, 0:2].reshape(96, 3, 128)]
    convert_element_type x1 -> x0, local copies, waits for them, and re-layouts: 5.59 us -> none  [fast_device(): g = g.reshape(4, 96, 2 * FF).astype(F32)]
    convert_element_type x1 -> x4, other arithmetic: 1.17 us -> 6.56 us  [the longest x1 2.75 us: fast_device(): ge_in.astype(F32)]
where the time goes in v2:
time: 272 us; the launch traced here: 271 us
  Pallas kernels  251 us (92%)
  other arithmetic  11.4 us (4%)
  local copies, waits for them, and re-layouts  7.69 us (3%)
    pallas_call x1, Pallas kernels, layer_call(): pl.pallas_call(functools.partial(layer_kernel, names), out_shape=[jax.Sha...  251 us

profile of v2, /device:TPU:0, one launch (start us, length us, event | category | flops | bytes accessed | tf_op | source)
XLA Modules:
  0.0 271.4 jit_solution(16696442711877676433)
XLA Ops:
  0.6 0.0 copy-start
  0.7 0.0 copy-start.10
  0.7 0.0 copy-start.11
  0.7 0.0 copy-start.8
  0.7 0.0 copy-start.9
  0.7 1.1 constant_dynamic-slice_fusion.1
  1.8 0.1 copy.37
  1.9 0.1 copy.38
  2.1 0.1 copy.39
  2.2 0.1 copy.40
  2.3 0.1 copy.41
  2.4 0.7 concatenate.7.refs_2_
  3.2 0.0 copy-done.10
  3.2 0.0 copy-done.11
  3.2 0.0 copy-done.8
  3.2 0.1 pad.11.clone
  3.3 0.1 maximum_maximum_fusion
  3.4 0.6 pad_convert_fusion.refs_3_
  4.0 0.0 copy-done
  4.0 0.6 dynamic-slice_convert_fusion.refs_4_
  4.6 0.0 copy-done.9
  4.6 0.8 fusion.2.refs_5_
  5.4 251.4 %layer.1 = (bf16[256,768]{1,0:T(8,128)(2,1)}, f32[256,768]{1,0:T(8,128)}, f32[8,768]{1,0:T(8,128)}, bf16[4,576,128]{2,1,0:T(8,128)(2,1)}, bf16[4,48,384]{2,1,0:T...) custom-call(bf16[256,768]{1,0:T(8,128)(2,1)} %bitcast.48, ...), custom_call_target="tpu_custom_call" | custom-call | flops 35000000512 | bytes 60000000 | tf_op jit(solution)/shard_map/layer/pallas_call | solution.py:1504
  256.9 0.0 copy-start.7
  256.9 0.0 copy-start.1
  256.9 2.8 %multiply_reduce_fusion = (f32[96]{0:T(128)S(1)}, f32[96,12,3,64]{0,3,2,1:T(8,128)}) fusion(f32[96,12,3,64]{0,3,2,1:T(8,128)} %param.17, bf16[12,3,64,128]{3,2,1,0:T(8,128)(2,1)} %bitcast.35), kind=kLoop, calls=%fused_computation.1 | loop fusion | flops 1105824 | bytes 2212224 | tf_op jit(solution)/shard_map/reduce_sum | solution.py:1585
  259.7 0.5 convert_divide_fusion
  260.3 0.0 copy-done.7
  260.3 0.2 copy.35
  260.4 0.7 copy.42
  261.2 0.8 constant_dynamic-slice_fusion
  262.0 0.5 slice_bitcast_fusion.1
  262.5 0.6 slice_bitcast_fusion
  263.0 0.0 copy-done.1
  263.0 0.0 copy-start.2
  263.1 2.7 %convert_element_type.65 = f32[3,96,4096]{2,1,0:T(8,128)} convert(bf16[3,96,4096]{2,1,0:T(8,128)(2,1)S(1)} %copy-done.1) | non-fusion elementwise | flops 1179648 | bytes 7077888 | tf_op jit(solution)/shard_map/convert_element_type | solution.py:1596
  265.8 0.0 copy-done.2
  265.8 0.0 copy-start.4
  265.8 1.6 convert_element_type.66
  267.4 0.0 copy-done.4
  267.4 0.0 copy-start.6
  267.4 1.3 convert_element_type.67
  268.7 0.0 copy-start.5
  268.7 0.0 copy-start.3
  268.7 0.0 copy-done.6
  268.7 0.9 convert_element_type.68
  269.6 0.2 copy-done.5
  269.8 0.7 copy.49
  270.5 0.0 copy-done.3
  270.5 0.9 copy.50
  (15 shorter events, 0.1 us)
Async XLA Ops:
  0.6 3.3 %copy-start = (f32[96,768]{1,0:T(8,128)S(1)}, f32[96,768]{1,0:T(8,128)}, u32[]{:S(2)}) copy-start(f32[96,768]{1,0:T(8,128)} %param.18) | copy-start | bytes 884740
  0.7 2.5 copy-start.10
  0.7 2.5 copy-start.11
  0.7 2.5 copy-start.8
  0.7 3.9 %copy-start.9 = (s32[1,256,2]{1,2,0:T(2,128)S(1)}, s32[1,256,2]{1,2,0:T(2,128)}, u32[]{:S(2)}) copy-start(s32[1,256,2]{1,2,0:T(2,128)} %param.25) | copy-start | bytes 6148
  256.9 3.4 %copy-start.7 = (bf16[4,48,384]{2,1,0:T(8,128)(2,1)S(1)}, bf16[4,48,384]{2,1,0:T(8,128)(2,1)}, u32[]{:S(2)}) copy-start(bf16[4,48,384]{2,1,0:T(8,128)(2,1)} %get-tuple-element.23) | copy-start | bytes 442372
  256.9 6.2 %copy-start.1 = (bf16[3,96,4096]{2,1,0:T(8,128)(2,1)S(1)}, bf16[3,96,4096]{2,1,0:T(8,128)(2,1)}, u32[]{:S(2)}) copy-start(bf16[3,96,4096]{2,1,0:T(8,128)(2,1)} %get-tuple-element.25) | copy-start | bytes 7077892
  263.0 2.8 %copy-start.2 = (bf16[3,256,768]{2,1,0:T(8,128)(2,1)S(1)}, bf16[3,256,768]{2,1,0:T(8,128)(2,1)}, u32[]{:S(2)}) copy-start(bf16[3,256,768]{2,1,0:T(8,128)(2,1)} %get-tuple-element.26) | copy-start | bytes 3538948
  265.8 1.6 copy-start.4
  267.4 1.3 copy-start.6
  268.7 1.1 copy-start.5
  268.7 1.8 copy-start.3

commit v3 on v2

--- a/solution.py
+++ b/solution.py
@@ -457,6 +457,8 @@
 F32 = jnp.float32
 TOK = ATT_BLOCK
 QKV_PAD = 640
+FAR3 = 5
+RSY0 = 5
 
 
 def nn(a, b):
@@ -495,6 +497,8 @@
     yp = (b + 1 - 2 * y, s)
     z0p = (b + 2 - 4 * z0, s)
     z1p = (b + 4 - 8 * z1, s)
+    inner = lax.div(z + 1, 2) == 1
+    zip_ = (b + 6 - 4 * z, s)
     p1 = (b + c * (2 - 4 * z0), s + (1 - c) * (2 - 4 * x))
     p2 = (b + (1 - c) * (2 - 4 * z0), s + c * (2 - 4 * x))
     jme = z0 * 2 + x
@@ -524,6 +528,10 @@
     def ag_first(src, slot, ss, rs):
         send(src, slot(z, y), ss(0), rs(b), z0p)
 
+        @pl.when(inner)
+        def _():
+            send(src, slot(z, y), ss(7), rs(b), zip_)
+
     def ag_own(slot, ss, rs):
         send(slot(z, y), slot(z, y), ss(1), rs(b), z1p)
         send(slot(z, y), slot(z, y), ss(2), rs(b), yp)
@@ -531,7 +539,11 @@
     def ag_z0(slot, ss, rs):
         k = 2 * zf + y
         got(slot(zf, y), rs(k))
-        send(slot(zf, y), slot(zf, y), ss(3), rs(k), z1p)
+
+        @pl.when(inner)
+        def _():
+            send(slot(zf, y), slot(zf, y), ss(3), rs(k), z1p)
+
         send(slot(zf, y), slot(zf, y), ss(4), rs(k), yp)
 
     def ag_z1(slot, ss, rs):
@@ -546,8 +558,13 @@
 
     def ag_sent(src, slot, ss):
         sent(src, ss(0))
-        for n in range(1, 7):
+        for n in (1, 2, 4, 5, 6):
             sent(slot(z, y), ss(n))
+
+        @pl.when(inner)
+        def _():
+            sent(slot(z, y), ss(3))
+            sent(src, ss(7))
 
     def tok_own(slot, n):
         own = slot(jme, c)
@@ -616,7 +633,7 @@
         return total
 
     barrier = pltpu.get_barrier_semaphore()
-    peers = (core, xp, diag, yp, z0p, z1p)
+    peers = (core, xp, diag, yp, z0p, z1p, zip_)
     for dev in peers:
         pl.semaphore_signal(barrier, inc=1, device_id=dev, device_id_type=MESH)
 
@@ -705,16 +722,8 @@
         ag_z0(slot, ss, rs)
     got(r.nall.at[xf], r.x_r.at[1])
     send(r.nall.at[xf], r.nall.at[xf], r.x_s.at[2], r.x_r.at[2], core)
-    for m in range(4):
+    def w_first(m):
         ag_first(r.dg.at[m, pl.ds(0, 96)], w_slot(m), w_ss(m), w_rs(m))
-    for src, slot, ss, rs in att_sets:
-        ag_z1(slot, ss, rs)
-    tok_own(sel_slot, 2)
-    tok_own(cot_slot, 0)
-    ag_first(*ow_set)
-    ag_own(*ow_set[1:])
-    for src, slot, ss, rs in att_sets:
-        ag_fin(slot, rs)
 
     def w_own(m):
         ag_own(w_slot(m), w_ss(m), w_rs(m))
@@ -745,16 +754,31 @@
             got(r.wout.at[m, 0], r.o_r.at[m, 0])
             got(r.wout.at[m, 1], r.o_r.at[m, 1])
 
-        for n in range(1, 7):
+        for n in (1, 2, 4, 5, 6):
             sent(r.win.at[m, z, y], r.w_s.at[m, n])
+
+        @pl.when(inner)
+        def _():
+            sent(r.win.at[m, z, y], r.w_s.at[m, 3])
 
         @pl.when(c == y)
         def _():
             for k in range(3):
                 sent(r.wout.at[m, 0], r.o_s.at[m, k])
 
+    w_first(0)
+    for src, slot, ss, rs in att_sets:
+        ag_z1(slot, ss, rs)
+    ag_first(*ow_set)
+    ag_own(*ow_set[1:])
+    tok_own(sel_slot, 2)
+    tok_own(cot_slot, 0)
+    w_first(1)
+    for src, slot, ss, rs in att_sets:
+        ag_fin(slot, rs)
+
     w_own(0)
-    w_own(1)
+    w_relay(0)
 
     rows = jnp.zeros((8, D), F32)
     for k in range(8):
@@ -798,10 +822,9 @@
     lax.fori_loop(0, 4, project, 0)
 
     ag_z0(*ow_set[1:])
-    w_own(2)
-    w_own(3)
-    for m in range(4):
-        w_relay(m)
+    w_own(1)
+    w_relay(1)
+    w_first(2)
     ag_z1(*ow_set[1:])
     tok_near(sel_slot, 2)
     tok_near(cot_slot, 0)
@@ -841,6 +864,7 @@
             w_relay_far(0)
             tok_far(sel_slot, 2)
             tok_far(cot_slot, 0)
+            w_first(3)
         if i == 0:
             w_relay_far(1)
 
@@ -1028,6 +1052,11 @@
     for m in range(4):
         sent(r.dg.at[m, pl.ds(0, 96)], r.w_s.at[m, 0])
 
+        @pl.when(inner)
+        def _(m=m):
+            sent(r.dg.at[m, pl.ds(0, 96)], r.w_s.at[m, 7])
+
+
     def arrive(p, carry):
         q = lax.div(p, 2)
         k2 = lax.rem(p, 2)
@@ -1037,14 +1066,14 @@
         @pl.when(p == 2)
         def _():
             tok_near(two_slot, 1)
+            w_own(2)
+            w_relay(2)
+            w_own(3)
+            w_relay(3)
 
         @pl.when(k2 == 1)
         def _():
             got(two_slot(j, k), r.tok_r.at[1, p])
-
-        @pl.when(p == 4)
-        def _():
-            w_relay_far(2)
 
         @pl.when(p == 5)
         def _():
@@ -1055,16 +1084,13 @@
         return carry
 
     lax.fori_loop(0, 8, arrive, 0)
+    w_relay_far(2)
     weight_grads(0)
     tok_sent(two_slot, 1)
     tok_sent(sel_slot, 2)
     tok_sent(cot_slot, 0)
 
     def feed(m, carry):
-        @pl.when(m == 1)
-        def _():
-            w_relay_far(3)
-
         w_fin(m)
 
         def each(p, inner):
@@ -1073,6 +1099,14 @@
             j = block_at(3 - lax.rem(p, 4))
             tokens(m, j, k)
 
+            @pl.when((m == 1) & (p == FAR3))
+            def _():
+                w_relay_far(3)
+
+            @pl.when((m == 2) & (p == RSY0))
+            def _():
+                rs_y(0)
+
             @pl.when(m == 3)
             def _():
                 pack(j, k)
@@ -1085,14 +1119,9 @@
 
         lax.fori_loop(0, 8, each, 0)
 
-        @pl.when(m == 2)
-        def _():
-            rs_y(0)
-
         @pl.when(m == 3)
         def _():
             sum_core(r.ngb, r.ng_c, r.ng_p, 0)
-            rs_y(1)
 
         weight_grads(m)
         return carry
@@ -1107,12 +1136,14 @@
 
     lax.fori_loop(0, 4, mix, 0)
     sum_relay(r.ngb, r.ng_p, 0)
+    rs_y(1)
+    rs_z(0)
     lax.fori_loop(4, 8, mix, 0)
     rs_y(2)
     out_c = r.ng_c.at[:, :, pl.ds(0, D)]
     out_p = r.ng_p.at[:, :, pl.ds(0, D)]
     ngs = sum_fin(r.ngb, r.ng_c, r.ng_p, 0)
-    rs_z(0)
+    rs_z(1)
 
     small_dev = (core, xp, yp, z1p, z0p)
 
@@ -1171,7 +1202,6 @@
         r.acc[i, 1, :, 0:D] = jnp.zeros((TOK, D), F32)
     small_add(0)
     rs_y(3)
-    rs_z(1)
     for i in range(4):
 
         @pl.when(s != i)
@@ -1179,6 +1209,7 @@
             got(r.dat.at[i], r.d_r.at[i])
             sent(r.att.at[i], r.d_s.at[i])
 
+    rs_join(0)
     sum_first(r.cota, out_c, 1)
 
     chunks = ((0, 128), (128, 256), (384, 256))
@@ -1291,7 +1322,7 @@
             head_ends(*chunks[0])
             q_first(0)
             og_core()
-            rs_join(0)
+            rs_join(1)
             sum_core(r.cota, out_c, out_p, 1)
             rs_z(2)
             small_add(1)
@@ -1303,8 +1334,9 @@
             og_xp()
             sum_relay(r.cota, out_p, 1)
             q_add_y(0)
-            rs_join(1)
+            rs_join(2)
             rs_spread(0)
+            rs_spread(1)
             small_add(2)
 
         @pl.when(h == 2)
@@ -1330,8 +1362,6 @@
     send(n_slot(2 - 2 * x + c), r.n_x, r.n_s.at[2], r.n_r.at[2], xp)
     q_add_z(0)
     rs_z(3)
-    rs_join(2)
-    rs_spread(1)
     rs_end(0)
     small_add(3)
     q_add_y(2)
@@ -1465,9 +1495,9 @@
         "small_o": vmem((5, 8, D), F32),
         "small_i": vmem((5, 8, D), F32),
         "stage_sem": dma((4, 9)),
-        "att_s": dma((3, 7)),
+        "att_s": dma((3, 8)),
         "att_r": dma((3, 8)),
-        "w_s": dma((4, 7)),
+        "w_s": dma((4, 8)),
         "w_r": dma((4, 8)),
         "o_s": dma((4, 3)),
         "o_r": dma((4, 2)),

time: 272 us -> 246 us (0.904)
  Pallas kernels: 251 us -> 225 us
    pallas_call x1, Pallas kernels: 251 us -> 225 us  [layer_call(): pl.pallas_call(functools.partial(layer_kernel, names), out_shape=[jax.Sha...]
where the time goes in v3:
time: 246 us; the launch traced here: 245 us
  Pallas kernels  225 us (91%)
  other arithmetic  11.4 us (5%)
  local copies, waits for them, and re-layouts  7.69 us (3%)
    pallas_call x1, Pallas kernels, layer_call(): pl.pallas_call(functools.partial(layer_kernel, names), out_shape=[jax.Sha...  225 us

profile of v3, /device:TPU:0, one launch (start us, length us, event | category | flops | bytes accessed | tf_op | source)
XLA Modules:
  0.0 245.1 jit_solution(16269112234787081643)
XLA Ops:
  0.6 0.0 copy-start
  0.7 0.0 copy-start.10
  0.7 0.0 copy-start.11
  0.7 0.0 copy-start.8
  0.7 0.0 copy-start.9
  0.7 1.1 constant_dynamic-slice_fusion.1
  1.8 0.1 copy.37
  1.9 0.1 copy.38
  2.1 0.1 copy.39
  2.2 0.1 copy.40
  2.3 0.1 copy.41
  2.4 0.7 concatenate.7.refs_2_
  3.2 0.0 copy-done.10
  3.2 0.0 copy-done.11
  3.2 0.0 copy-done.8
  3.2 0.1 pad.11.clone
  3.3 0.1 maximum_maximum_fusion
  3.4 0.6 pad_convert_fusion.refs_3_
  4.0 0.0 copy-done
  4.0 0.6 dynamic-slice_convert_fusion.refs_4_
  4.6 0.0 copy-done.9
  4.6 0.8 fusion.2.refs_5_
  5.4 225.2 %layer.1 = (bf16[256,768]{1,0:T(8,128)(2,1)}, f32[256,768]{1,0:T(8,128)}, f32[8,768]{1,0:T(8,128)}, bf16[4,576,128]{2,1,0:T(8,128)(2,1)}, bf16[4,48,384]{2,1,0:T...) custom-call(bf16[256,768]{1,0:T(8,128)(2,1)} %bitcast.48, ...), custom_call_target="tpu_custom_call" | custom-call | flops 35000000512 | bytes 60000000 | tf_op jit(solution)/shard_map/layer/pallas_call | solution.py:1534
  230.6 0.0 copy-start.7
  230.6 0.0 copy-start.1
  230.6 2.8 %multiply_reduce_fusion = (f32[96]{0:T(128)S(1)}, f32[96,12,3,64]{0,3,2,1:T(8,128)}) fusion(f32[96,12,3,64]{0,3,2,1:T(8,128)} %param.17, bf16[12,3,64,128]{3,2,1,0:T(8,128)(2,1)} %bitcast.35), kind=kLoop, calls=%fused_computation.1 | loop fusion | flops 1105824 | bytes 2212224 | tf_op jit(solution)/shard_map/reduce_sum | solution.py:1615
  233.5 0.5 convert_divide_fusion
  234.0 0.0 copy-done.7
  234.0 0.2 copy.35
  234.2 0.7 copy.42
  234.9 0.8 constant_dynamic-slice_fusion
  235.7 0.5 slice_bitcast_fusion.1
  236.2 0.6 slice_bitcast_fusion
  236.8 0.0 copy-done.1
  236.8 0.0 copy-start.2
  236.8 2.7 %convert_element_type.65 = f32[3,96,4096]{2,1,0:T(8,128)} convert(bf16[3,96,4096]{2,1,0:T(8,128)(2,1)S(1)} %copy-done.1) | non-fusion elementwise | flops 1179648 | bytes 7077888 | tf_op jit(solution)/shard_map/convert_element_type | solution.py:1626
  239.5 0.0 copy-done.2
  239.5 0.0 copy-start.4
  239.5 1.6 convert_element_type.66
  241.1 0.0 copy-done.4
  241.1 0.0 copy-start.6
  241.1 1.3 convert_element_type.67
  242.4 0.0 copy-start.5
  242.4 0.0 copy-start.3
  242.4 0.0 copy-done.6
  242.4 0.9 convert_element_type.68
  243.4 0.2 copy-done.5
  243.5 0.7 copy.49
  244.3 0.0 copy-done.3
  244.3 0.9 copy.50
  (15 shorter events, 0.1 us)
Async XLA Ops:
  0.6 3.3 %copy-start = (f32[96,768]{1,0:T(8,128)S(1)}, f32[96,768]{1,0:T(8,128)}, u32[]{:S(2)}) copy-start(f32[96,768]{1,0:T(8,128)} %param.18) | copy-start | bytes 884740
  0.7 2.5 %copy-start.10 = (f32[96]{0:T(128)S(1)}, f32[96]{0:T(128)}, u32[]{:S(2)}) copy-start(f32[96]{0:T(128)} %param.19) | copy-start | bytes 1156
  0.7 2.5 %copy-start.11 = (f32[96]{0:T(128)S(1)}, f32[96]{0:T(128)}, u32[]{:S(2)}) copy-start(f32[96]{0:T(128)} %param.16) | copy-start | bytes 1156
  0.7 2.5 %copy-start.8 = (f32[96,3]{0,1:T(4,128)S(1)}, f32[96,3]{0,1:T(4,128)}, u32[]{:S(2)}) copy-start(f32[96,3]{0,1:T(4,128)} %param.20) | copy-start | bytes 3460
  0.7 3.9 %copy-start.9 = (s32[1,256,2]{1,2,0:T(2,128)S(1)}, s32[1,256,2]{1,2,0:T(2,128)}, u32[]{:S(2)}) copy-start(s32[1,256,2]{1,2,0:T(2,128)} %param.25) | copy-start | bytes 6148
  230.6 3.4 %copy-start.7 = (bf16[4,48,384]{2,1,0:T(8,128)(2,1)S(1)}, bf16[4,48,384]{2,1,0:T(8,128)(2,1)}, u32[]{:S(2)}) copy-start(bf16[4,48,384]{2,1,0:T(8,128)(2,1)} %get-tuple-element.23) | copy-start | bytes 442372
  230.6 6.2 %copy-start.1 = (bf16[3,96,4096]{2,1,0:T(8,128)(2,1)S(1)}, bf16[3,96,4096]{2,1,0:T(8,128)(2,1)}, u32[]{:S(2)}) copy-start(bf16[3,96,4096]{2,1,0:T(8,128)(2,1)} %get-tuple-element.25) | copy-start | bytes 7077892
  236.8 2.8 %copy-start.2 = (bf16[3,256,768]{2,1,0:T(8,128)(2,1)S(1)}, bf16[3,256,768]{2,1,0:T(8,128)(2,1)}, u32[]{:S(2)}) copy-start(bf16[3,256,768]{2,1,0:T(8,128)(2,1)} %get-tuple-element.26) | copy-start | bytes 3538948
  239.5 1.6 copy-start.4
  241.1 1.3 copy-start.6
  242.4 1.1 copy-start.5
  242.4 1.8 copy-start.3

commit v4 on v3

--- a/solution.py
+++ b/solution.py
@@ -704,6 +704,55 @@
         ag_first(src, slot, ss, rs)
         ag_own(slot, ss, rs)
 
+    xf = s + 2 - 4 * x
+    for src, slot, ss, rs in att_sets:
+        ag_z0(slot, ss, rs)
+    got(r.nall.at[xf], r.x_r.at[1])
+    send(r.nall.at[xf], r.nall.at[xf], r.x_s.at[2], r.x_r.at[2], core)
+    def w_first(m):
+        ag_first(r.dg.at[m, pl.ds(0, 96)], w_slot(m), w_ss(m), w_rs(m))
+
+    def w_own(m):
+        ag_own(w_slot(m), w_ss(m), w_rs(m))
+
+        @pl.when(c == y)
+        def _():
+            v = r.wout.at[m, z1]
+            send(v, v, r.o_s.at[m, 0], r.o_r.at[m, z1], z1p)
+            send(v, v, r.o_s.at[m, 1], r.o_r.at[m, z1], yp)
+
+    def w_relay(m):
+        ag_z0(w_slot(m), w_ss(m), w_rs(m))
+
+    def w_relay_far(m):
+        ag_z1(w_slot(m), w_ss(m), w_rs(m))
+
+        @pl.when(c == y)
+        def _():
+            v = r.wout.at[m, 1 - z1]
+            got(v, r.o_r.at[m, 1 - z1])
+            send(v, v, r.o_s.at[m, 2], r.o_r.at[m, 1 - z1], yp)
+
+    def w_fin(m):
+        ag_fin(w_slot(m), w_rs(m))
+
+        @pl.when(c != y)
+        def _():
+            got(r.wout.at[m, 0], r.o_r.at[m, 0])
+            got(r.wout.at[m, 1], r.o_r.at[m, 1])
+
+        for n in (1, 2, 4, 5, 6):
+            sent(r.win.at[m, z, y], r.w_s.at[m, n])
+
+        @pl.when(inner)
+        def _():
+            sent(r.win.at[m, z, y], r.w_s.at[m, 3])
+
+        @pl.when(c == y)
+        def _():
+            for k in range(3):
+                sent(r.wout.at[m, 0], r.o_s.at[m, k])
+
     for one in staged:
         one.wait()
     for m in range(4):
@@ -716,55 +765,6 @@
     def _():
         for m in range(4):
             r.wout[m, z1] = r.acc[m // 2, m % 2, 96:224, 0:D].astype(BF)
-
-    xf = s + 2 - 4 * x
-    for src, slot, ss, rs in att_sets:
-        ag_z0(slot, ss, rs)
-    got(r.nall.at[xf], r.x_r.at[1])
-    send(r.nall.at[xf], r.nall.at[xf], r.x_s.at[2], r.x_r.at[2], core)
-    def w_first(m):
-        ag_first(r.dg.at[m, pl.ds(0, 96)], w_slot(m), w_ss(m), w_rs(m))
-
-    def w_own(m):
-        ag_own(w_slot(m), w_ss(m), w_rs(m))
-
-        @pl.when(c == y)
-        def _():
-            v = r.wout.at[m, z1]
-            send(v, v, r.o_s.at[m, 0], r.o_r.at[m, z1], z1p)
-            send(v, v, r.o_s.at[m, 1], r.o_r.at[m, z1], yp)
-
-    def w_relay(m):
-        ag_z0(w_slot(m), w_ss(m), w_rs(m))
-
-    def w_relay_far(m):
-        ag_z1(w_slot(m), w_ss(m), w_rs(m))
-
-        @pl.when(c == y)
-        def _():
-            v = r.wout.at[m, 1 - z1]
-            got(v, r.o_r.at[m, 1 - z1])
-            send(v, v, r.o_s.at[m, 2], r.o_r.at[m, 1 - z1], yp)
-
-    def w_fin(m):
-        ag_fin(w_slot(m), w_rs(m))
-
-        @pl.when(c != y)
-        def _():
-            got(r.wout.at[m, 0], r.o_r.at[m, 0])
-            got(r.wout.at[m, 1], r.o_r.at[m, 1])
-
-        for n in (1, 2, 4, 5, 6):
-            sent(r.win.at[m, z, y], r.w_s.at[m, n])
-
-        @pl.when(inner)
-        def _():
-            sent(r.win.at[m, z, y], r.w_s.at[m, 3])
-
-        @pl.when(c == y)
-        def _():
-            for k in range(3):
-                sent(r.wout.at[m, 0], r.o_s.at[m, k])
 
     w_first(0)
     for src, slot, ss, rs in att_sets:

time: 246 us -> 246 us (level)
  no operation moved by 1% of the time
where the time goes in v4:
time: 246 us; the launch traced here: 245 us
  Pallas kernels  225 us (91%)
  other arithmetic  11.4 us (5%)
  local copies, waits for them, and re-layouts  7.69 us (3%)
    pallas_call x1, Pallas kernels, layer_call(): pl.pallas_call(functools.partial(layer_kernel, names), out_shape=[jax.Sha...  225 us

profile of v4, /device:TPU:0, one launch (start us, length us, event | category | flops | bytes accessed | tf_op | source)
XLA Modules:
  0.0 245.1 jit_solution(18160052237344290890)
XLA Ops:
  0.6 0.0 copy-start
  0.7 0.0 copy-start.10
  0.7 0.0 copy-start.11
  0.7 0.0 copy-start.8
  0.7 0.0 copy-start.9
  0.7 1.1 constant_dynamic-slice_fusion.1
  1.8 0.1 copy.37
  1.9 0.1 copy.38
  2.1 0.1 copy.39
  2.2 0.1 copy.40
  2.3 0.1 copy.41
  2.4 0.7 concatenate.7.refs_2_
  3.2 0.0 copy-done.10
  3.2 0.0 copy-done.11
  3.2 0.0 copy-done.8
  3.2 0.1 pad.11.clone
  3.3 0.1 maximum_maximum_fusion
  3.4 0.6 pad_convert_fusion.refs_3_
  4.0 0.0 copy-done
  4.0 0.6 dynamic-slice_convert_fusion.refs_4_
  4.6 0.0 copy-done.9
  4.6 0.8 fusion.2.refs_5_
  5.4 225.1 %layer.1 = (bf16[256,768]{1,0:T(8,128)(2,1)}, f32[256,768]{1,0:T(8,128)}, f32[8,768]{1,0:T(8,128)}, bf16[4,576,128]{2,1,0:T(8,128)(2,1)}, bf16[4,48,384]{2,1,0:T...) custom-call(bf16[256,768]{1,0:T(8,128)(2,1)} %bitcast.48, ...), custom_call_target="tpu_custom_call" | custom-call | flops 35000000512 | bytes 60000000 | tf_op jit(solution)/shard_map/layer/pallas_call | solution.py:1534
  230.5 0.0 copy-start.7
  230.5 0.0 copy-start.1
  230.5 2.8 %multiply_reduce_fusion = (f32[96]{0:T(128)S(1)}, f32[96,12,3,64]{0,3,2,1:T(8,128)}) fusion(f32[96,12,3,64]{0,3,2,1:T(8,128)} %param.17, bf16[12,3,64,128]{3,2,1,0:T(8,128)(2,1)} %bitcast.35), kind=kLoop, calls=%fused_computation.1 | loop fusion | flops 1105824 | bytes 2212224 | tf_op jit(solution)/shard_map/reduce_sum | solution.py:1615
  233.4 0.5 convert_divide_fusion
  233.9 0.0 copy-done.7
  233.9 0.2 copy.35
  234.1 0.7 copy.42
  234.8 0.8 constant_dynamic-slice_fusion
  235.6 0.5 slice_bitcast_fusion.1
  236.1 0.6 slice_bitcast_fusion
  236.7 0.0 copy-done.1
  236.7 0.0 copy-start.2
  236.7 2.7 %convert_element_type.65 = f32[3,96,4096]{2,1,0:T(8,128)} convert(bf16[3,96,4096]{2,1,0:T(8,128)(2,1)S(1)} %copy-done.1) | non-fusion elementwise | flops 1179648 | bytes 7077888 | tf_op jit(solution)/shard_map/convert_element_type | solution.py:1626
  239.4 0.0 copy-done.2
  239.4 0.0 copy-start.4
  239.4 1.6 convert_element_type.66
  241.1 0.0 copy-done.4
  241.1 0.0 copy-start.6
  241.1 1.3 convert_element_type.67
  242.3 0.0 copy-start.5
  242.3 0.0 copy-start.3
  242.3 0.0 copy-done.6
  242.3 0.9 convert_element_type.68
  243.3 0.2 copy-done.5
  243.4 0.7 copy.49
  244.2 0.0 copy-done.3
  244.2 0.9 copy.50
  (15 shorter events, 0.1 us)
Async XLA Ops:
  0.6 3.3 %copy-start = (f32[96,768]{1,0:T(8,128)S(1)}, f32[96,768]{1,0:T(8,128)}, u32[]{:S(2)}) copy-start(f32[96,768]{1,0:T(8,128)} %param.18) | copy-start | bytes 884740
  0.7 2.5 %copy-start.10 = (f32[96]{0:T(128)S(1)}, f32[96]{0:T(128)}, u32[]{:S(2)}) copy-start(f32[96]{0:T(128)} %param.19) | copy-start | bytes 1156
  0.7 2.5 %copy-start.11 = (f32[96]{0:T(128)S(1)}, f32[96]{0:T(128)}, u32[]{:S(2)}) copy-start(f32[96]{0:T(128)} %param.16) | copy-start | bytes 1156
  0.7 2.5 %copy-start.8 = (f32[96,3]{0,1:T(4,128)S(1)}, f32[96,3]{0,1:T(4,128)}, u32[]{:S(2)}) copy-start(f32[96,3]{0,1:T(4,128)} %param.20) | copy-start | bytes 3460
  0.7 3.9 %copy-start.9 = (s32[1,256,2]{1,2,0:T(2,128)S(1)}, s32[1,256,2]{1,2,0:T(2,128)}, u32[]{:S(2)}) copy-start(s32[1,256,2]{1,2,0:T(2,128)} %param.25) | copy-start | bytes 6148
  230.5 3.4 %copy-start.7 = (bf16[4,48,384]{2,1,0:T(8,128)(2,1)S(1)}, bf16[4,48,384]{2,1,0:T(8,128)(2,1)}, u32[]{:S(2)}) copy-start(bf16[4,48,384]{2,1,0:T(8,128)(2,1)} %get-tuple-element.23) | copy-start | bytes 442372
  230.5 6.2 %copy-start.1 = (bf16[3,96,4096]{2,1,0:T(8,128)(2,1)S(1)}, bf16[3,96,4096]{2,1,0:T(8,128)(2,1)}, u32[]{:S(2)}) copy-start(bf16[3,96,4096]{2,1,0:T(8,128)(2,1)} %get-tuple-element.25) | copy-start | bytes 7077892
  236.7 2.8 %copy-start.2 = (bf16[3,256,768]{2,1,0:T(8,128)(2,1)S(1)}, bf16[3,256,768]{2,1,0:T(8,128)(2,1)}, u32[]{:S(2)}) copy-start(bf16[3,256,768]{2,1,0:T(8,128)(2,1)} %get-tuple-element.26) | copy-start | bytes 3538948
  239.4 1.6 copy-start.4
  241.1 1.3 copy-start.6
  242.3 1.1 copy-start.5
  242.3 1.8 copy-start.3
